TPU v7x, 256 devices: a whole 4x4x8 slice. The times are simulated.
256 devices in a mesh: expert: 16 (over z, core), panel: 16 (over x, y).
Axes of the slice: x: 4, y: 4, z: 8, core: 2. Of those that a mesh axis runs over, the one named last changes fastest.
Arguments:
- queries: bfloat16 [2048, 4, 7168], P('expert', None, 'panel'), may hold values from -6 to 6
- expert_ids: int32 [2048, 4], P('expert'), may hold values from 0 to 15, all different within a row; in each aligned block of 128 rows (0 to 127, 128 to 255, ...) at most 64 rows name the same one
- mix_weights: float32 [2048, 4], P('expert'), may hold values from 0.2 to 1
- factors: bfloat16 [16, 7168, 7168], P('expert', 'panel'), as said below
Outputs:
- combined: bfloat16 [2048, 7168], P('expert', 'panel')
Inputs may be any that keep to these rules, and one draw needn't show every extreme that they name: `expert_ids`: each token names 4 different experts; the 128 tokens held at one position along `expert` send at most 64 rows to any one expert, and some expert receives exactly 64 of them. `factors`: each expert's factor is symmetric.
All inputs are finite; a program needn't handle non-finite values.
Results may differ from a plain program's by a relative error of at most 0.005.
Values may be sent and summed in bfloat16 or wider, within the bound.
No kernel may reach another device: no remote copies, remote signals or barrier semaphores. Data moves between devices by JAX's collectives and lax.ppermute only.
A program may use at most 192 MiB of HBM per device.

v0:
```python
import jax
import jax.numpy as jnp
from jax import lax
from jax.sharding import PartitionSpec as P


def on_device(queries, expert_ids, mix_weights, factors):
    groups = lax.axis_size("expert")
    tokens_here, top_count, feat_here = queries.shape
    row_total = tokens_here * top_count
    capacity = 2 * row_total // groups
    flat_ids = expert_ids.reshape(row_total)
    onehot = (flat_ids[:, None] == jnp.arange(groups, dtype=jnp.int32)[None, :]).astype(jnp.int32)
    position = jnp.sum(jnp.cumsum(onehot, axis=0) * onehot, axis=1) - 1
    target = flat_ids * capacity + position
    outgoing = jnp.zeros((groups * capacity, feat_here), queries.dtype)
    outgoing = outgoing.at[target].set(queries.reshape(row_total, feat_here))
    arrived = lax.all_to_all(
        outgoing.reshape(groups, capacity, feat_here),
        "expert",
        split_axis=0,
        concat_axis=0,
        tiled=True,
    )
    arrived = arrived.reshape(groups * capacity, feat_here)
    panel_rows = factors[0]
    result = lax.psum_scatter(
        lax.dot_general(
            panel_rows, arrived, (((0,), (1,)), ((), ())), preferred_element_type=jnp.float32
        ),
        "panel",
        scatter_dimension=0,
        tiled=True,
    ).T
    precond = result.astype(jnp.bfloat16).reshape(groups, capacity, feat_here)
    returned = lax.all_to_all(precond, "expert", split_axis=0, concat_axis=0, tiled=True)
    returned = returned.reshape(groups * capacity, feat_here)
    picked = returned[target].reshape(tokens_here, top_count, feat_here).astype(jnp.float32)
    combined = jnp.sum(picked * mix_weights[:, :, None], axis=1)
    return combined.astype(jnp.bfloat16)


def solution(mesh):
    in_specs = (
        P("expert", None, "panel"),
        P("expert", None),
        P("expert", None),
        P("expert", "panel", None),
    )
    out_specs = P("expert", "panel")
    return jax.shard_map(
        on_device, mesh=mesh, in_specs=in_specs, out_specs=out_specs, check_vma=False
    )
```

profile of v0, /device:TPU:1, one launch (start us, length us, event | category | flops | bytes accessed | tf_op | source)
XLA Modules:
  0.0 323.9 jit_solution(14150870023071836215)
XLA Ops:
  6.5 0.0 reduce-scatter.4.cloned.1.call-start
  6.5 0.8 copy.20
  7.3 0.1 eq.29
  7.4 0.1 eq.25
  7.5 0.7 broadcast_multiply_fusion
  8.2 1.1 reduce-window.6
  9.4 0.2 slice_reduce_fusion
  9.6 0.1 fusion.4
  9.8 0.1 copy.19
  9.9 0.1 mul.29
  10.0 1.4 copy.23
  11.4 0.3 reshape.89
  11.7 2.7 scatter_custom_fusion
  14.4 38.3 %all_to_all.10 = bf16[16,64,448]{2,1,0:T(8,128)(2,1)S(1)} all-to-all(bf16[16,64,448]{2,1,0:T(8,128)(2,1)S(1)} %bitcast.31), channel_id=1, replica_groups=mesh['expert'=16,'panel'=16] {'expert'}, dimensions={0} | all-to-all | bytes 1835008 | tf_op jit(solution)/shard_map/all_to_all | solution.py:18
  52.8 16.3 %convolution_bitcast_fusion = f32[7168,1024]{0,1:T(8,128)} fusion(bf16[1024,448]{1,0:T(8,128)(2,1)S(1)} %bitcast.32, bf16[1,448,7168]{2,1,0:T(8,128)(2,1)} %param.7), kind=kOutput, calls=%fused_computation.2 | convolution fusion | flops 6576668672 | bytes 36700160 | tf_op jit(solution)/shard_map/dot_general | solution.py:28
  69.0 29.5 %copy.26 = f32[7168,1024]{1,0:T(8,128)} copy(f32[7168,1024]{0,1:T(8,128)} %convolution_bitcast_fusion) | data formatting | bytes 58720256
  98.6 0.0 copy-start
  98.6 0.0 reduce-scatter.4.cloned.1.call-update
  98.6 176.7 %reduce-scatter.4.cloned.1.call-done = f32[448,1024]{1,0:T(8,128)} async-done(((f32[7168,1024]{1,0:T(8,128)}), f32[448,1024]{1,0:T(8,128)}) %reduce-scatter.4.cloned.1.call-update) | async-done | bytes 1835024
  275.2 2.5 copy.27
  277.7 7.7 %all-to-all-start.1 = ((bf16[16,64,448]{2,1,0:T(8,128)(2,1)}), bf16[16,64,448]{2,1,0:T(8,128)(2,1)S(1)}, u32[]{:S(2)}, u32[]{:S(2)}) async-start(bf16[16,64,448]{2,1,0:T(8,128)(2,1)} %bitcast.8), calls=%async_computation.1 | async-start | bytes 2097152 | tf_op jit(solution)/shard_map/all_to_all | solution.py:36
  285.4 0.0 copy-done
  285.4 0.1 copy.24
  285.5 27.8 %all-to-all-done.1 = bf16[16,64,448]{2,1,0:T(8,128)(2,1)S(1)} async-done(((bf16[16,64,448]{2,1,0:T(8,128)(2,1)}), bf16[16,64,448]{2,1,0:T(8,128)(2,1)S(1)}, u32[]{:S(2)}, u32[]{:S(2)}) %all-to-all-start.1) | async-done | bytes 917536 | tf_op jit(solution)/shard_map/all_to_all | solution.py:36
  313.3 2.0 gather_fusion
  315.3 0.3 reshape.76
  315.6 0.7 multiply_reduce_fusion
  316.3 0.8 copy.25
  (6 shorter events, 0.1 us)
Async XLA Ops:
  6.5 268.7 %reduce-scatter.4.cloned.1.call-start = ((), (), s32[]{:S(2)}) async-start(), calls=%async_computation.3 | async-start | bytes 31195136
  98.6 186.8 %copy-start = (f32[128,4]{0,1:T(4,128)S(1)}, f32[128,4]{0,1:T(4,128)}, u32[]{:S(2)}) copy-start(f32[128,4]{0,1:T(4,128)} %param.6) | copy-start | bytes 6148
  277.7 35.6 %all-to-all-start.1 = ((bf16[16,64,448]{2,1,0:T(8,128)(2,1)}), bf16[16,64,448]{2,1,0:T(8,128)(2,1)S(1)}, u32[]{:S(2)}, u32[]{:S(2)}) async-start(bf16[16,64,448]{2,1,0:T(8,128)(2,1)} %bitcast.8), calls=%async_computation.1 | async-start | bytes 2097152 | tf_op jit(solution)/shard_map/all_to_all | solution.py:36
Sparse Core Ops, SparseCore 0:
  98.7 176.4 reduce-scatter.3
where the time goes:
time: 325 us; the launch traced here: 324 us
  waiting for transfers between devices  204 us (63%)
  local copies, waits for them, and re-layouts  41 us (13%)
  blocking collectives  38.3 us (12%)
  matrix products  16.3 us (5%)
  between operations  13.5 us (4%)
  starting transfers between devices  7.66 us (2%)
    unnamed x2, waiting for transfers between devices  177 us
    all_to_all x1, blocking collectives, on_device(): lax.all_to_all(outgoing.reshape(groups, capacity, feat_here), 'expert', s...  38.3 us
    unnamed x7, local copies, waits for them, and re-layouts  34.3 us
    all_to_all x1, waiting for transfers between devices, on_device(): lax.all_to_all(precond, 'expert', split_axis=0, concat_axis=0, tiled=True)  27.8 us
    dot_general x1, matrix products, on_device(): lax.dot_general(panel_rows, arrived, (((0,), (1,)), ((), ())), preferred_...  16.3 us
    all_to_all x1, starting transfers between devices, on_device(): lax.all_to_all(precond, 'expert', split_axis=0, concat_axis=0, tiled=True)  7.66 us
  transfers between devices with their start and end apart: 2, of which 2 were waited for; matrix products, arithmetic and copies ran while one was open for 0% of the time, Pallas kernels for 0%

commit v1 on v0

v1 whole, which is shorter than its diff:
```python
import functools

import jax
import jax.numpy as jnp
from jax import lax
from jax.experimental import pallas as pl
from jax.experimental.pallas import tpu as pltpu
from jax.sharding import PartitionSpec as P

SIDE = 4
CHIPS = 8
SLOTS = 64
WIDE = 2 * SLOTS
X_FIRST = (2, 6, 3, 5)
Y_FIRST = (0, 1, 7, 4)
WINDOW = 512
STEPS = (0, -1, 1, 2)
VMEM = 50 * 1024 * 1024


def along_x(by):
    return [(x * SIDE + y, (x + by) % SIDE * SIDE + y) for x in range(SIDE) for y in range(SIDE)]


def along_y(by):
    return [(x * SIDE + y, x * SIDE + (y + by) % SIDE) for x in range(SIDE) for y in range(SIDE)]


def along_z(by):
    return [(z * 2 + c, (z + by) % CHIPS * 2 + c) for z in range(CHIPS) for c in range(2)]


SWAP = [(i, i ^ 1) for i in range(2 * CHIPS)]


def dot(a, b, dims=((1,), (0,))):
    return lax.dot_general(a, b, (dims, ((), ())), preferred_element_type=jnp.float32)


def route_kernel(own_ids, own_mix, own_rows, other_ids, other_mix, other_rows, *rest):
    blocks, (high, low), (turned, chosen) = rest[:CHIPS], rest[CHIPS : CHIPS + 2], rest[CHIPS + 2 :]
    me = lax.axis_index("expert")
    z, core = me // 2, me % 2
    top_count, tokens, _ = own_rows.shape
    width = CHIPS * WIDE
    lane = lax.broadcasted_iota(jnp.int32, (tokens, width), 1)
    earlier = (
        lax.broadcasted_iota(jnp.int32, (tokens, tokens), 0)
        > lax.broadcasted_iota(jnp.int32, (tokens, tokens), 1)
    ).astype(jnp.bfloat16)
    experts = lax.broadcasted_iota(jnp.int32, (tokens, 2 * CHIPS), 1)
    sides = (own_ids, own_mix, own_rows), (other_ids, other_mix, other_rows)
    for n, (ids, mix, rows) in enumerate(sides):
        source = core if n == 0 else 1 - core
        ids, mix = ids[...].T, mix[...].T
        named = [ids[:, j : j + 1] for j in range(top_count)]
        hits = [(experts == one).astype(jnp.float32) for one in named]
        before = dot(earlier, sum(hits).astype(jnp.bfloat16))
        weights = jnp.zeros((tokens, width), jnp.float32)
        for j in range(top_count):
            slot = jnp.sum(hits[j] * before, axis=1, keepdims=True).astype(jnp.int32)
            shift = ((named[j] >> 1) - z + CHIPS) & (CHIPS - 1)
            place = jnp.where((named[j] & 1) == core, shift * WIDE + source * SLOTS + slot, -1)
            taken = lane == place
            span = pl.ds((n * top_count + j) * tokens, tokens)
            chosen[span, :] = taken.astype(jnp.float32).astype(jnp.bfloat16)
            turned[:, span] = rows[j].T
            weights = jnp.where(taken, mix[:, j : j + 1], weights)
        upper = weights.astype(jnp.bfloat16)
        high[pl.ds(n * tokens, tokens), :] = upper
        low[pl.ds(n * tokens, tokens), :] = (weights - upper.astype(jnp.float32)).astype(jnp.bfloat16)
    for k in range(0, CHIPS, 2):
        pair = dot(turned[...], chosen[:, k * WIDE : (k + 2) * WIDE]).astype(jnp.bfloat16)
        blocks[k][...] = pair[:, :WIDE]
        blocks[k + 1][...] = pair[:, WIDE:]


def route(own, other):
    top_count, tokens, feat = own[2].shape
    width = CHIPS * WIDE
    outs = [jax.ShapeDtypeStruct((feat, WIDE), jnp.bfloat16)] * CHIPS
    outs += [jax.ShapeDtypeStruct((2 * tokens, width), jnp.bfloat16)] * 2
    got = pl.pallas_call(
        route_kernel,
        out_shape=outs,
        scratch_shapes=[
            pltpu.VMEM((feat, 2 * top_count * tokens), jnp.bfloat16),
            pltpu.VMEM((2 * top_count * tokens, width), jnp.bfloat16),
        ],
        compiler_params=pltpu.CompilerParams(vmem_limit_bytes=VMEM),
        name="route",
    )(*own, *other)
    return got[:CHIPS], got[CHIPS], got[CHIPS + 1]


def ring_kernel(x_first, early, factor, *rest):
    sources, rest = rest[: 3 if early else 2], rest[3 if early else 2 :]
    before, outs, (held, gathered, sems) = rest[:-3][: 1 - early], rest[1 - early : -3], rest[-3:]
    panel = lax.axis_index("panel")
    x, y = panel // SIDE, panel % SIDE
    feat, half = held.shape[1], held.shape[1] // 2
    width = gathered.shape[2]
    copies = []
    for g, second in enumerate(range(SIDE - 1) if early else (SIDE - 1,)):
        for first in range(SIDE):
            dx, dy = (STEPS[first], STEPS[second]) if x_first else (STEPS[second], STEPS[first])
            owner = (x + dx + SIDE) % SIDE * SIDE + (y + dy + SIDE) % SIDE
            lead = owner % 2 * (WINDOW - feat)
            top = first * WINDOW
            gathered[g, pl.ds(top, WINDOW - feat), :] = jnp.zeros((WINDOW - feat, width), gathered.dtype)
            gathered[g, pl.ds(top + feat, WINDOW - feat), :] = jnp.zeros((WINDOW - feat, width), gathered.dtype)
            columns = pl.ds(pl.multiple_of(owner * feat - lead, 128), WINDOW)
            window = held.at[g, :, pl.ds(top, WINDOW)]
            copies.append(pltpu.make_async_copy(factor.at[:, columns], window, sems.at[len(copies)]))
            copies[-1].start()
            for j in range(2):
                source = sources[second].at[j, first] if early else sources[j].at[first]
                target = gathered.at[g, pl.ds(pl.multiple_of(top + j * half + lead, 16), half)]
                copies.append(pltpu.make_async_copy(source, target, sems.at[len(copies)]))
                copies[-1].start()
    count = len(copies) // held.shape[0]
    for g in range(held.shape[0]):
        for copy in copies[g * count : (g + 1) * count]:
            copy.wait()
        total = dot(held[g], gathered[g])
        if early:
            outs[0][...] = total if g == 0 else total + outs[0][...]
    if not early:
        total = (total + before[0][...]).astype(jnp.bfloat16)
        for b, block in enumerate(outs):
            block[...] = total[:, b * WIDE : (b + 1) * WIDE]


def times_ring(factor, x_first, pieces, before=()):
    feat, full = factor.shape
    width = pieces[0].shape[-1]
    early = not before
    groups = SIDE - 1 if early else 1
    anywhere, vmem = pl.BlockSpec(memory_space=pl.ANY), pl.BlockSpec(memory_space=pltpu.VMEM)
    if early:
        outs = [jax.ShapeDtypeStruct((feat, width), jnp.float32)]
    else:
        outs = [jax.ShapeDtypeStruct((feat, WIDE), jnp.bfloat16)] * (width // WIDE)
    depth = SIDE * WINDOW
    return pl.pallas_call(
        functools.partial(ring_kernel, x_first, early),
        in_specs=[anywhere] * (1 + len(pieces)) + [vmem] * len(before),
        out_specs=[vmem] * len(outs),
        out_shape=outs,
        scratch_shapes=[
            pltpu.VMEM((groups, feat, depth), jnp.bfloat16),
            pltpu.VMEM((groups, depth, width), jnp.bfloat16),
            pltpu.SemaphoreType.DMA((groups * SIDE * 3,)),
        ],
        compiler_params=pltpu.CompilerParams(vmem_limit_bytes=VMEM),
        cost_estimate=pl.CostEstimate(
            flops=2 * groups * feat * depth * width,
            bytes_accessed=2 * groups * depth * (feat + width),
            transcendentals=0,
        ),
        name="times_ring_early" if early else "times_ring_late",
    )(factor, *pieces, *before)


def go_round(parts, way):
    behind, ahead = (lax.ppermute(parts, "panel", way(by)) for by in (1, -1))
    return behind, ahead, lax.ppermute(behind[0], "panel", way(1)), lax.ppermute(ahead[1], "panel", way(-1))


def ring_product(factor, block, x_first):
    feat, width = block.shape
    ways = (along_x, along_y) if x_first else (along_y, along_x)
    mine = block.reshape(2, feat // 2, width)
    behind, ahead, *across = go_round(mine, ways[0])
    line = jnp.stack([jnp.stack([mine[j], behind[j], ahead[j], across[j]]) for j in range(2)])
    behind, ahead, *across = go_round(line, ways[1])
    early = times_ring(factor, x_first, [line, behind, ahead])
    return times_ring(factor, x_first, across, early)


def combine_kernel(count, high, low, *rest):
    returned, (own, other) = rest[:count], rest[count:]
    tokens = own.shape[0]
    total = None
    for k, block in enumerate(returned):
        span = pl.ds(k * WIDE, WIDE)
        for part in (high, low):
            term = dot(part[:, span], block[...], ((1,), (1,)))
            total = term if total is None else total + term
    own[...] = total[:tokens]
    other[...] = total[tokens:]


def combine(high, low, returned):
    feat = returned[0].shape[0]
    return pl.pallas_call(
        functools.partial(combine_kernel, len(returned)),
        out_shape=[jax.ShapeDtypeStruct((high.shape[0] // 2, feat), jnp.float32)] * 2,
        compiler_params=pltpu.CompilerParams(vmem_limit_bytes=VMEM),
        name="combine",
    )(high, low, *returned)


def on_device(queries, expert_ids, mix_weights, factors):
    swap = lambda a: lax.ppermute(a, "expert", SWAP)
    mine = expert_ids.T, mix_weights.T, jnp.transpose(queries, (1, 0, 2))
    blocks, high, low = route(mine, tuple(map(swap, mine)))
    arrived = {k: lax.ppermute(blocks[k], "expert", along_z(k)) if k else blocks[k] for k in range(CHIPS)}

    product = {}
    for shifts in (X_FIRST, Y_FIRST):
        block = jnp.concatenate([arrived[k] for k in shifts], 1)
        product |= dict(zip(shifts, ring_product(factors[0], block, shifts is X_FIRST)))

    returned = [lax.ppermute(product[k], "expert", along_z(-k)) if k else product[k] for k in range(CHIPS)]
    own, other = combine(high, low, returned)
    return (own + swap(other)).astype(jnp.bfloat16)


def solution(mesh):
    in_specs = (
        P("expert", None, "panel"),
        P("expert", None),
        P("expert", None),
        P("expert", "panel", None),
    )
    out_specs = P("expert", "panel")
    return jax.shard_map(
        on_device, mesh=mesh, in_specs=in_specs, out_specs=out_specs, check_vma=False
    )
```

time: 325 us -> 164 us (0.50)
  waiting for transfers between devices: 204 us -> 68.1 us
  starting transfers between devices: 7.66 us -> 61.1 us
  blocking collectives: 38.3 us -> 0 us
  local copies, waits for them, and re-layouts: 41 us -> 6.7 us
  Pallas kernels: 0 us -> 26.3 us
  matrix products: 16.3 us -> 0 us
  between operations: 13.5 us -> 0.32 us
    unnamed x2 -> x0, waiting for transfers between devices: 177 us -> none
    ppermute x0 -> x34, waiting for transfers between devices: none -> 68.1 us  [the longest x8 43.4 us: go_round(): behind, ahead = (lax.ppermute(parts, 'panel', way(by)) for by in (1, -1))]
    ppermute x0 -> x34, starting transfers between devices: none -> 61.1 us  [the longest x7 16.3 us: on_device(): lax.ppermute(blocks[k], 'expert', along_z(k))]
    all_to_all x1 -> x0, blocking collectives: 38.3 us -> none  [on_device(): lax.all_to_all(outgoing.reshape(groups, capacity, feat_here), 'expert', s...]
    unnamed x7 -> x19, local copies, waits for them, and re-layouts: 34.3 us -> 4.17 us
    all_to_all x1 -> x0, waiting for transfers between devices: 27.8 us -> none  [on_device(): lax.all_to_all(precond, 'expert', split_axis=0, concat_axis=0, tiled=True)]
    pallas_call x0 -> x6, Pallas kernels: none -> 26.3 us  [the longest x4 22.2 us: times_ring(): pl.pallas_call(functools.partial(ring_kernel, x_first, early), in_specs=[...]
    dot_general x1 -> x0, matrix products: 16.3 us -> none  [on_device(): lax.dot_general(panel_rows, arrived, (((0,), (1,)), ((), ())), preferred_...]
  transfers between devices with their start and end apart: 2 -> 34, of which waited for: 2 -> 15; matrix products, arithmetic and copies ran while one was open for 0% -> 2% of each run, Pallas kernels for 0% -> 14%
where the time goes in v1:
time: 164 us; the launch traced here: 163 us
  waiting for transfers between devices  68.1 us (42%)
  starting transfers between devices  61.1 us (37%)
  Pallas kernels  26.3 us (16%)
  local copies, waits for them, and re-layouts  6.7 us (4%)
    ppermute x8, waiting for transfers between devices, go_round(): behind, ahead = (lax.ppermute(parts, 'panel', way(by)) for by in (1, -1))  43.4 us
    pallas_call x4, Pallas kernels, times_ring(): pl.pallas_call(functools.partial(ring_kernel, x_first, early), in_specs=[...  22.2 us
    ppermute x7, starting transfers between devices, on_device(): lax.ppermute(blocks[k], 'expert', along_z(k))  16.3 us
    ppermute x7, starting transfers between devices, on_device(): lax.ppermute(product[k], 'expert', along_z(-k))  14.7 us
    ppermute x8, starting transfers between devices, go_round(): behind, ahead = (lax.ppermute(parts, 'panel', way(by)) for by in (1, -1))  11.4 us
    ppermute x7, waiting for transfers between devices, on_device(): lax.ppermute(product[k], 'expert', along_z(-k))  10.2 us
    ppermute x4, starting transfers between devices, go_round(): lax.ppermute(ahead[1], 'panel', way(-1))  9.73 us
    ppermute x4, starting transfers between devices, on_device(): swap = lambda a: lax.ppermute(a, 'expert', SWAP)  7.37 us
  transfers between devices with their start and end apart: 34, of which 15 were waited for; matrix products, arithmetic and copies ran while one was open for 2% of the time, Pallas kernels for 14%

profile of v1, /device:TPU:1, one launch (start us, length us, event | category | flops | bytes accessed | tf_op | source)
XLA Modules:
  0.0 163.3 jit_solution(5484221649959887771)
XLA Ops:
  0.0 1.2 copy.5
  1.2 3.3 %collective-permute-start.2 = (bf16[4,128,448]{2,1,0:T(8,128)(2,1)S(1)}, bf16[4,128,448]{2,1,0:T(8,128)(2,1)S(1)}, u32[]{:S(2)}, u32[]{:S(2)}) collective-permute-start(bf16[4,128,448]{2,1,0:T(8,128)(2,1)S(1)} %bitcast.42), channel_id=1, source_target_pairs={{0,16},{16,0},{32,48},{48,32},{64,80},{80,64},{96,112},{112,96},{1... | collective-permute-start | bytes 1376264 | tf_op jit(solution)/shard_map/ppermute | solution.py:205
  4.6 0.1 collective-permute-start
  4.7 0.4 collective-permute-start.1
  5.1 1.2 collective-permute-done.other_ids
  6.3 0.7 copy-done
  7.0 0.7 copy-done.1
  7.7 2.8 %route.1 = (bf16[448,128]{1,0:T(8,128)(2,1)S(1)}, bf16[448,128]{1,0:T(8,128)(2,1)S(1)}, bf16[448,128]{1,0:T(8,128)(2,1)S(1)}, bf16[448,128]{1,0:T(8,128)(2,1)S(1...) custom-call(s32[4,128]{1,0:T(4,128)S(1)} %bitcast.45, ...), custom_call_target="tpu_custom_call" | custom-call | tf_op jit(solution)/shard_map/route/pallas_call | solution.py:83
  10.5 1.3 collective-permute-start.15
  11.8 3.1 %collective-permute-start.16 = (bf16[448,128]{1,0:T(8,128)(2,1)S(1)}, bf16[448,128]{1,0:T(8,128)(2,1)S(1)}, u32[]{:S(2)}, u32[]{:S(2)}) collective-permute-start(bf16[448,128]{1,0:T(8,128)(2,1)S(1)} %get-tuple-element.34), channel_id=1, source_target_pairs={{0,192},{16,208},{32,224},{48,240},{64,0},{80,16},{96,32},{112,48}... | collective-permute-start | bytes 344072 | tf_op jit(solution)/shard_map/ppermute | solution.py:208
  14.9 1.5 collective-permute-start.17
  16.5 2.9 %collective-permute-start.18 = (bf16[448,128]{1,0:T(8,128)(2,1)S(1)}, bf16[448,128]{1,0:T(8,128)(2,1)S(1)}, u32[]{:S(2)}, u32[]{:S(2)}) collective-permute-start(bf16[448,128]{1,0:T(8,128)(2,1)S(1)} %get-tuple-element.36), channel_id=1, source_target_pairs={{0,160},{16,176},{32,192},{48,208},{64,224},{80,240},{96,0},{112,1... | collective-permute-start | bytes 344072 | tf_op jit(solution)/shard_map/ppermute | solution.py:208
  19.4 0.7 collective-permute-start.3
  20.2 2.0 %collective-permute-start.4 = (bf16[448,128]{1,0:T(8,128)(2,1)S(1)}, bf16[448,128]{1,0:T(8,128)(2,1)S(1)}, u32[]{:S(2)}, u32[]{:S(2)}) collective-permute-start(bf16[448,128]{1,0:T(8,128)(2,1)S(1)} %get-tuple-element.29), channel_id=1, source_target_pairs={{0,224},{16,240},{32,0},{48,16},{64,32},{80,48},{96,64},{112,80},{... | collective-permute-start | bytes 344072 | tf_op jit(solution)/shard_map/ppermute | solution.py:208
  22.2 0.3 collective-permute-done.16
  22.5 4.6 %collective-permute-start.5 = (bf16[448,128]{1,0:T(8,128)(2,1)S(1)}, bf16[448,128]{1,0:T(8,128)(2,1)S(1)}, u32[]{:S(2)}, u32[]{:S(2)}) collective-permute-start(bf16[448,128]{1,0:T(8,128)(2,1)S(1)} %get-tuple-element.30), channel_id=1, source_target_pairs={{0,128},{16,144},{32,160},{48,176},{64,192},{80,208},{96,224},{112... | collective-permute-start | bytes 344072 | tf_op jit(solution)/shard_map/ppermute | solution.py:208
  27.1 1.6 collective-permute-done.17
  28.8 1.3 collective-permute-start.19
  30.1 1.5 collective-permute-start.20
  31.6 0.5 collective-permute-done.4
  32.1 3.0 %collective-permute-done.5 = bf16[448,128]{1,0:T(8,128)(2,1)S(1)} collective-permute-done((bf16[448,128]{1,0:T(8,128)(2,1)S(1)}, bf16[448,128]{1,0:T(8,128)(2,1)S(1)}, u32[]{:S(2)}, u32[]{:S(2)}) %collective-permute-start.5) | collective-permute-done | bytes 114720 | tf_op jit(solution)/shard_map/ppermute | solution.py:208
  35.1 1.4 collective-permute-start.6
  36.5 1.7 %collective-permute-start.7 = (bf16[2,224,512]{2,1,0:T(8,128)(2,1)S(1)}, bf16[2,224,512]{2,1,0:T(8,128)(2,1)S(1)}, u32[]{:S(2)}, u32[]{:S(2)}) collective-permute-start(bf16[2,224,512]{2,1,0:T(8,128)(2,1)S(1)} %bitcast.53), channel_id=1, source_target_pairs={{0,3},{1,0},{2,1},{3,2},{4,7},{5,4},{6,5},{7,6},{8,11},{9,8},{10,9... | collective-permute-start | bytes 1376264 | tf_op jit(solution)/shard_map/ppermute | solution.py:166
  38.3 2.0 %collective-permute-done.19 = bf16[2,224,512]{2,1,0:T(8,128)(2,1)S(1)} collective-permute-done((bf16[2,224,512]{2,1,0:T(8,128)(2,1)S(1)}, bf16[2,224,512]{2,1,0:T(8,128)(2,1)S(1)}, u32[]{:S(2)}, u32[]{:S(2)}) %collective-permute-start.19) | collective-permute-done | bytes 458784 | tf_op jit(solution)/shard_map/ppermute | solution.py:166
  40.3 0.1 collective-permute-start.21
  40.5 2.7 %collective-permute-start.22 = (bf16[224,512]{1,0:T(8,128)(2,1)S(1)}, bf16[224,512]{1,0:T(8,128)(2,1)S(1)}, u32[]{:S(2)}, u32[]{:S(2)}) collective-permute-start(bf16[224,512]{1,0:T(8,128)(2,1)S(1)} %get-tuple-element.51), channel_id=1, source_target_pairs={{0,12},{1,13},{2,14},{3,15},{4,0},{5,1},{6,2},{7,3},{8,4},{9,5},{1... | collective-permute-start | bytes 688136 | tf_op jit(solution)/shard_map/ppermute | solution.py:167
  43.2 4.6 %collective-permute-done.6 = bf16[2,224,512]{2,1,0:T(8,128)(2,1)S(1)} collective-permute-done((bf16[2,224,512]{2,1,0:T(8,128)(2,1)S(1)}, bf16[2,224,512]{2,1,0:T(8,128)(2,1)S(1)}, u32[]{:S(2)}, u32[]{:S(2)}) %collective-permute-start.6) | collective-permute-done | bytes 458784 | tf_op jit(solution)/shard_map/ppermute | solution.py:166
  48.0 2.8 %collective-permute-start.9 = (bf16[224,512]{1,0:T(8,128)(2,1)S(1)}, bf16[224,512]{1,0:T(8,128)(2,1)S(1)}, u32[]{:S(2)}, u32[]{:S(2)}) collective-permute-start(bf16[224,512]{1,0:T(8,128)(2,1)S(1)} %get-tuple-element.59), channel_id=1, source_target_pairs={{0,3},{1,0},{2,1},{3,2},{4,7},{5,4},{6,5},{7,6},{8,11},{9,8},{10,9... | collective-permute-start | bytes 688136 | tf_op jit(solution)/shard_map/ppermute | solution.py:167
  50.8 0.1 maximum_bitcast_fusion.2
  50.9 0.1 maximum_bitcast_fusion.3
  51.0 0.2 pad_maximum_fusion.1.rest_0_
  51.4 2.7 %collective-permute-start.25 = (bf16[2,4,224,512]{3,2,1,0:T(8,128)(2,1)S(1)}, bf16[2,4,224,512]{3,2,1,0:T(8,128)(2,1)S(1)}, u32[]{:S(2)}, u32[]{:S(2)}) collective-permute-start(bf16[2,4,224,512]{3,2,1,0:T(8,128)(2,1)S(1)} %pad_maximum_fusion.1.rest_0_), channel_id=1, source_target_pairs={{0,3},{1,0},{2,1},{3,2},{4,7},{5,4},{6,5},{7,6},{8,11},{9,8},{10,9... | collective-permute-start | bytes 5505032 | tf_op jit(solution)/shard_map/ppermute | solution.py:166
  54.1 0.5 collective-permute-done.8
  54.6 0.1 maximum_bitcast_fusion
  54.7 0.1 maximum_bitcast_fusion.1
  54.8 0.2 pad_maximum_fusion.rest_0_
  55.0 1.2 collective-permute-start.10
  56.2 1.5 collective-permute-start.12
  57.8 36.8 %collective-permute-done.23.rest_1_ = bf16[2,4,224,512]{3,2,1,0:T(8,128)(2,1)S(1)} collective-permute-done((bf16[2,4,224,512]{3,2,1,0:T(8,128)(2,1)S(1)}, bf16[2,4,224,512]{3,2,1,0:T(8,128)(2,1)S(1)}, u32[]{:S(2)}, u32[]{:S(2)}) %collective-permute-start.23) | collective-permute-done | bytes 1835040 | tf_op jit(solution)/shard_map/ppermute | solution.py:166
  94.8 1.3 slice_bitcast_fusion
  96.0 0.1 copy-done.2
  96.2 2.4 %collective-permute-start.26 = (bf16[4,224,512]{2,1,0:T(8,128)(2,1)}, bf16[4,224,512]{2,1,0:T(8,128)(2,1)S(1)}, u32[]{:S(2)}, u32[]{:S(2)}) collective-permute-start(bf16[4,224,512]{2,1,0:T(8,128)(2,1)} %slice_bitcast_fusion), channel_id=1, source_target_pairs={{0,3},{1,0},{2,1},{3,2},{4,7},{5,4},{6,5},{7,6},{8,11},{9,8},{10,9... | collective-permute-start | bytes 2752520 | tf_op jit(solution)/shard_map/ppermute | solution.py:167
  98.6 1.3 copy-done.4
  99.9 1.2 collective-permute-start.11
  101.2 1.8 %collective-permute-start.13 = (bf16[4,224,512]{2,1,0:T(8,128)(2,1)S(1)}, bf16[4,224,512]{2,1,0:T(8,128)(2,1)S(1)}, u32[]{:S(2)}, u32[]{:S(2)}) collective-permute-start(bf16[4,224,512]{2,1,0:T(8,128)(2,1)S(1)} %slice_bitcast_fusion.2), channel_id=1, source_target_pairs={{0,12},{1,13},{2,14},{3,15},{4,0},{5,1},{6,2},{7,3},{8,4},{9,5},{1... | collective-permute-start | bytes 2752520 | tf_op jit(solution)/shard_map/ppermute | solution.py:167
  103.0 7.0 %times_ring_early.3.rest_2_ = f32[448,512]{1,0:T(8,128)S(1)} custom-call(bf16[448,7168]{1,0:T(8,128)(2,1)} %bitcast.48, bf16[2,4,224,512]{3,2,1,0:T(8,128)(2,1)S(1)} %pad_maximum_fusion.1.rest_0_, bf16[2,4,224,512]{3,2,1,0:T(8,128)(2,1)} %copy-done.2, bf16[2,4,224,512]{3,2,1,0:T(8,128)(2,1)} %copy-done.3), custom_call_target="tpu_custom_call" | custom-call | flops 2818572288 | bytes 11796480 | tf_op jit(solution)/shard_map/times_ring_early/pallas_call | solution.py:145
  110.1 5.8 %collective-permute-done.24.rest_0_ = bf16[4,224,512]{2,1,0:T(8,128)(2,1)S(1)} collective-permute-done((bf16[4,224,512]{2,1,0:T(8,128)(2,1)S(1)}, bf16[4,224,512]{2,1,0:T(8,128)(2,1)S(1)}, u32[]{:S(2)}, u32[]{:S(2)}) %collective-permute-start.24) | collective-permute-done | bytes 917536 | tf_op jit(solution)/shard_map/ppermute | solution.py:167
  115.9 0.5 collective-permute-done.26.rest_1_
  116.4 4.1 %times_ring_late.3 = (bf16[448,128]{1,0:T(8,128)(2,1)S(1)}, bf16[448,128]{1,0:T(8,128)(2,1)S(1)}, bf16[448,128]{1,0:T(8,128)(2,1)S(1)}, bf16[448,128]{1,0:T(8,128)(2,1)S(1)}) custom-call(bf16[448,7168]{1,0:T(8,128)(2,1)} %bitcast.49, bf16[4,224,512]{2,1,0:T(8,128)(2,1)S(1)} %collective-permute-done.24.rest_0_, ...), custom_call_target="tpu_custom_call" | custom-call | flops 939524096 | bytes 3932160 | tf_op jit(solution)/shard_map/times_ring_late/pallas_call | solution.py:145
  120.5 4.6 %collective-permute-start.27 = (bf16[448,128]{1,0:T(8,128)(2,1)S(1)}, bf16[448,128]{1,0:T(8,128)(2,1)S(1)}, u32[]{:S(2)}, u32[]{:S(2)}) collective-permute-start(bf16[448,128]{1,0:T(8,128)(2,1)S(1)} %get-tuple-element.37), channel_id=1, source_target_pairs={{0,192},{16,208},{32,224},{48,240},{64,0},{80,16},{96,32},{112,48}... | collective-permute-start | bytes 344072 | tf_op jit(solution)/shard_map/ppermute | solution.py:215
  125.1 1.0 collective-permute-start.28
  126.1 7.0 %times_ring_early.2.rest_2_ = f32[448,512]{1,0:T(8,128)S(1)} custom-call(bf16[448,7168]{1,0:T(8,128)(2,1)} %bitcast.50, bf16[2,4,224,512]{3,2,1,0:T(8,128)(2,1)S(1)} %pad_maximum_fusion.rest_0_, bf16[2,4,224,512]{3,2,1,0:T(8,128)(2,1)} %copy-done.4, bf16[2,4,224,512]{3,2,1,0:T(8,128)(2,1)} %copy-done.5), custom_call_target="tpu_custom_call" | custom-call | flops 2818572288 | bytes 11796480 | tf_op jit(solution)/shard_map/times_ring_early/pallas_call | solution.py:145
  133.1 2.3 %collective-permute-start.30 = (bf16[448,128]{1,0:T(8,128)(2,1)S(1)}, bf16[448,128]{1,0:T(8,128)(2,1)S(1)}, u32[]{:S(2)}, u32[]{:S(2)}) collective-permute-start(bf16[448,128]{1,0:T(8,128)(2,1)S(1)} %get-tuple-element.40), channel_id=1, source_target_pairs={{0,96},{16,112},{32,128},{48,144},{64,160},{80,176},{96,192},{112,... | collective-permute-start | bytes 344072 | tf_op jit(solution)/shard_map/ppermute | solution.py:215
  135.5 0.1 collective-permute-start.31
  135.6 4.1 %times_ring_late.2 = (bf16[448,128]{1,0:T(8,128)(2,1)S(1)}, bf16[448,128]{1,0:T(8,128)(2,1)S(1)}, bf16[448,128]{1,0:T(8,128)(2,1)S(1)}, bf16[448,128]{1,0:T(8,128)(2,1)S(1)}) custom-call(bf16[448,7168]{1,0:T(8,128)(2,1)} %bitcast.51, bf16[4,224,512]{2,1,0:T(8,128)(2,1)S(1)} %collective-permute-done.11.rest_0_, ...), custom_call_target="tpu_custom_call" | custom-call | flops 939524096 | bytes 3932160 | tf_op jit(solution)/shard_map/times_ring_late/pallas_call | solution.py:145
  139.7 4.6 %collective-permute-start.14 = (bf16[448,128]{1,0:T(8,128)(2,1)S(1)}, bf16[448,128]{1,0:T(8,128)(2,1)S(1)}, u32[]{:S(2)}, u32[]{:S(2)}) collective-permute-start(bf16[448,128]{1,0:T(8,128)(2,1)S(1)} %get-tuple-element.32), channel_id=1, source_target_pairs={{0,224},{16,240},{32,0},{48,16},{64,32},{80,48},{96,64},{112,80},{... | collective-permute-start | bytes 344072 | tf_op jit(solution)/shard_map/ppermute | solution.py:215
  144.4 2.0 %collective-permute-start.29 = (bf16[448,128]{1,0:T(8,128)(2,1)S(1)}, bf16[448,128]{1,0:T(8,128)(2,1)S(1)}, u32[]{:S(2)}, u32[]{:S(2)}) collective-permute-start(bf16[448,128]{1,0:T(8,128)(2,1)S(1)} %get-tuple-element.39), channel_id=1, source_target_pairs={{0,128},{16,144},{32,160},{48,176},{64,192},{80,208},{96,224},{112... | collective-permute-start | bytes 344072 | tf_op jit(solution)/shard_map/ppermute | solution.py:215
  146.4 1.7 %collective-permute-done.31.rest_6_ = bf16[448,128]{1,0:T(8,128)(2,1)S(1)} collective-permute-done((bf16[448,128]{1,0:T(8,128)(2,1)S(1)}, bf16[448,128]{1,0:T(8,128)(2,1)S(1)}, u32[]{:S(2)}, u32[]{:S(2)}) %collective-permute-start.31) | collective-permute-done | bytes 114720 | tf_op jit(solution)/shard_map/ppermute | solution.py:215
  148.1 6.1 %collective-permute-done.29.rest_4_ = bf16[448,128]{1,0:T(8,128)(2,1)S(1)} collective-permute-done((bf16[448,128]{1,0:T(8,128)(2,1)S(1)}, bf16[448,128]{1,0:T(8,128)(2,1)S(1)}, u32[]{:S(2)}, u32[]{:S(2)}) %collective-permute-start.29) | collective-permute-done | bytes 114720 | tf_op jit(solution)/shard_map/ppermute | solution.py:215
  154.3 2.3 %collective-permute-done.32.rest_7_ = bf16[448,128]{1,0:T(8,128)(2,1)S(1)} collective-permute-done((bf16[448,128]{1,0:T(8,128)(2,1)S(1)}, bf16[448,128]{1,0:T(8,128)(2,1)S(1)}, u32[]{:S(2)}, u32[]{:S(2)}) %collective-permute-start.32) | collective-permute-done | bytes 114720 | tf_op jit(solution)/shard_map/ppermute | solution.py:215
  156.6 1.2 combine.1
  157.8 3.5 %collective-permute-start.33 = (f32[128,448]{1,0:T(8,128)S(1)}, f32[128,448]{1,0:T(8,128)S(1)}, u32[]{:S(2)}, u32[]{:S(2)}) collective-permute-start(f32[128,448]{1,0:T(8,128)S(1)} %get-tuple-element.44), channel_id=1, source_target_pairs={{0,16},{16,0},{32,48},{48,32},{64,80},{80,64},{96,112},{112,96},{1... | collective-permute-start | bytes 688136 | tf_op jit(solution)/shard_map/ppermute | solution.py:205
  161.3 1.2 collective-permute-done.33
  162.5 0.8 copy.6
  (49 shorter events, 1.0 us)
Async XLA Ops:
  1.2 5.1 %collective-permute-start.2 = (bf16[4,128,448]{2,1,0:T(8,128)(2,1)S(1)}, bf16[4,128,448]{2,1,0:T(8,128)(2,1)S(1)}, u32[]{:S(2)}, u32[]{:S(2)}) collective-permute-start(bf16[4,128,448]{2,1,0:T(8,128)(2,1)S(1)} %bitcast.42), channel_id=1, source_target_pairs={{0,16},{16,0},{32,48},{48,32},{64,80},{80,64},{96,112},{112,96},{1... | collective-permute-start | bytes 1376264 | tf_op jit(solution)/shard_map/ppermute | solution.py:205
  4.6 1.8 %collective-permute-start = (s32[4,128]{1,0:T(4,128)}, s32[4,128]{1,0:T(4,128)S(1)}, u32[]{:S(2)}, u32[]{:S(2)}) collective-permute-start(s32[4,128]{1,0:T(4,128)} %bitcast.44), channel_id=1, source_target_pairs={{0,16},{16,0},{32,48},{48,32},{64,80},{80,64},{96,112},{112,96},{1... | collective-permute-start | bytes 6152 | tf_op jit(solution)/shard_map/ppermute | solution.py:205
  4.7 1.7 %collective-permute-start.1 = (f32[4,128]{1,0:T(4,128)}, f32[4,128]{1,0:T(4,128)S(1)}, u32[]{:S(2)}, u32[]{:S(2)}) collective-permute-start(f32[4,128]{1,0:T(4,128)} %bitcast.46), channel_id=1, source_target_pairs={{0,16},{16,0},{32,48},{48,32},{64,80},{80,64},{96,112},{112,96},{1... | collective-permute-start | bytes 6152 | tf_op jit(solution)/shard_map/ppermute | solution.py:205
  6.3 0.7 copy-start
  7.0 0.7 copy-start.1
  10.5 9.7 %collective-permute-start.15 = (bf16[448,128]{1,0:T(8,128)(2,1)S(1)}, bf16[448,128]{1,0:T(8,128)(2,1)S(1)}, u32[]{:S(2)}, u32[]{:S(2)}) collective-permute-start(bf16[448,128]{1,0:T(8,128)(2,1)S(1)} %get-tuple-element.33), channel_id=1, source_target_pairs={{0,64},{16,80},{32,96},{48,112},{64,128},{80,144},{96,160},{112,17... | collective-permute-start | bytes 344072 | tf_op jit(solution)/shard_map/ppermute | solution.py:208
  11.8 10.7 %collective-permute-start.16 = (bf16[448,128]{1,0:T(8,128)(2,1)S(1)}, bf16[448,128]{1,0:T(8,128)(2,1)S(1)}, u32[]{:S(2)}, u32[]{:S(2)}) collective-permute-start(bf16[448,128]{1,0:T(8,128)(2,1)S(1)} %get-tuple-element.34), channel_id=1, source_target_pairs={{0,192},{16,208},{32,224},{48,240},{64,0},{80,16},{96,32},{112,48}... | collective-permute-start | bytes 344072 | tf_op jit(solution)/shard_map/ppermute | solution.py:208
  14.9 13.8 %collective-permute-start.17 = (bf16[448,128]{1,0:T(8,128)(2,1)S(1)}, bf16[448,128]{1,0:T(8,128)(2,1)S(1)}, u32[]{:S(2)}, u32[]{:S(2)}) collective-permute-start(bf16[448,128]{1,0:T(8,128)(2,1)S(1)} %get-tuple-element.35), channel_id=1, source_target_pairs={{0,96},{16,112},{32,128},{48,144},{64,160},{80,176},{96,192},{112,... | collective-permute-start | bytes 344072 | tf_op jit(solution)/shard_map/ppermute | solution.py:208
  16.5 12.3 %collective-permute-start.18 = (bf16[448,128]{1,0:T(8,128)(2,1)S(1)}, bf16[448,128]{1,0:T(8,128)(2,1)S(1)}, u32[]{:S(2)}, u32[]{:S(2)}) collective-permute-start(bf16[448,128]{1,0:T(8,128)(2,1)S(1)} %get-tuple-element.36), channel_id=1, source_target_pairs={{0,160},{16,176},{32,192},{48,208},{64,224},{80,240},{96,0},{112,1... | collective-permute-start | bytes 344072 | tf_op jit(solution)/shard_map/ppermute | solution.py:208
  19.4 12.1 %collective-permute-start.3 = (bf16[448,128]{1,0:T(8,128)(2,1)S(1)}, bf16[448,128]{1,0:T(8,128)(2,1)S(1)}, u32[]{:S(2)}, u32[]{:S(2)}) collective-permute-start(bf16[448,128]{1,0:T(8,128)(2,1)S(1)} %get-tuple-element.28), channel_id=1, source_target_pairs={{0,32},{16,48},{32,64},{48,80},{64,96},{80,112},{96,128},{112,144}... | collective-permute-start | bytes 344072 | tf_op jit(solution)/shard_map/ppermute | solution.py:208
  20.2 11.9 %collective-permute-start.4 = (bf16[448,128]{1,0:T(8,128)(2,1)S(1)}, bf16[448,128]{1,0:T(8,128)(2,1)S(1)}, u32[]{:S(2)}, u32[]{:S(2)}) collective-permute-start(bf16[448,128]{1,0:T(8,128)(2,1)S(1)} %get-tuple-element.29), channel_id=1, source_target_pairs={{0,224},{16,240},{32,0},{48,16},{64,32},{80,48},{96,64},{112,80},{... | collective-permute-start | bytes 344072 | tf_op jit(solution)/shard_map/ppermute | solution.py:208
  22.5 12.6 %collective-permute-start.5 = (bf16[448,128]{1,0:T(8,128)(2,1)S(1)}, bf16[448,128]{1,0:T(8,128)(2,1)S(1)}, u32[]{:S(2)}, u32[]{:S(2)}) collective-permute-start(bf16[448,128]{1,0:T(8,128)(2,1)S(1)} %get-tuple-element.30), channel_id=1, source_target_pairs={{0,128},{16,144},{32,160},{48,176},{64,192},{80,208},{96,224},{112... | collective-permute-start | bytes 344072 | tf_op jit(solution)/shard_map/ppermute | solution.py:208
  28.8 11.5 %collective-permute-start.19 = (bf16[2,224,512]{2,1,0:T(8,128)(2,1)S(1)}, bf16[2,224,512]{2,1,0:T(8,128)(2,1)S(1)}, u32[]{:S(2)}, u32[]{:S(2)}) collective-permute-start(bf16[2,224,512]{2,1,0:T(8,128)(2,1)S(1)} %bitcast.54), channel_id=1, source_target_pairs={{0,4},{1,5},{2,6},{3,7},{4,8},{5,9},{6,10},{7,11},{8,12},{9,13},{1... | collective-permute-start | bytes 1376264 | tf_op jit(solution)/shard_map/ppermute | solution.py:166
  30.1 10.3 %collective-permute-start.20 = (bf16[2,224,512]{2,1,0:T(8,128)(2,1)S(1)}, bf16[2,224,512]{2,1,0:T(8,128)(2,1)S(1)}, u32[]{:S(2)}, u32[]{:S(2)}) collective-permute-start(bf16[2,224,512]{2,1,0:T(8,128)(2,1)S(1)} %bitcast.55), channel_id=1, source_target_pairs={{0,12},{1,13},{2,14},{3,15},{4,0},{5,1},{6,2},{7,3},{8,4},{9,5},{1... | collective-permute-start | bytes 1376264 | tf_op jit(solution)/shard_map/ppermute | solution.py:166
  35.1 12.7 %collective-permute-start.6 = (bf16[2,224,512]{2,1,0:T(8,128)(2,1)S(1)}, bf16[2,224,512]{2,1,0:T(8,128)(2,1)S(1)}, u32[]{:S(2)}, u32[]{:S(2)}) collective-permute-start(bf16[2,224,512]{2,1,0:T(8,128)(2,1)S(1)} %bitcast.52), channel_id=1, source_target_pairs={{0,1},{1,2},{2,3},{3,0},{4,5},{5,6},{6,7},{7,4},{8,9},{9,10},{10,1... | collective-permute-start | bytes 1376264 | tf_op jit(solution)/shard_map/ppermute | solution.py:166
  36.5 11.4 %collective-permute-start.7 = (bf16[2,224,512]{2,1,0:T(8,128)(2,1)S(1)}, bf16[2,224,512]{2,1,0:T(8,128)(2,1)S(1)}, u32[]{:S(2)}, u32[]{:S(2)}) collective-permute-start(bf16[2,224,512]{2,1,0:T(8,128)(2,1)S(1)} %bitcast.53), channel_id=1, source_target_pairs={{0,3},{1,0},{2,1},{3,2},{4,7},{5,4},{6,5},{7,6},{8,11},{9,8},{10,9... | collective-permute-start | bytes 1376264 | tf_op jit(solution)/shard_map/ppermute | solution.py:166
  40.3 10.5 %collective-permute-start.21 = (bf16[224,512]{1,0:T(8,128)(2,1)S(1)}, bf16[224,512]{1,0:T(8,128)(2,1)S(1)}, u32[]{:S(2)}, u32[]{:S(2)}) collective-permute-start(bf16[224,512]{1,0:T(8,128)(2,1)S(1)} %get-tuple-element.48), channel_id=1, source_target_pairs={{0,4},{1,5},{2,6},{3,7},{4,8},{5,9},{6,10},{7,11},{8,12},{9,13},{1... | collective-permute-start | bytes 688136 | tf_op jit(solution)/shard_map/ppermute | solution.py:167
  40.5 10.5 %collective-permute-start.22 = (bf16[224,512]{1,0:T(8,128)(2,1)S(1)}, bf16[224,512]{1,0:T(8,128)(2,1)S(1)}, u32[]{:S(2)}, u32[]{:S(2)}) collective-permute-start(bf16[224,512]{1,0:T(8,128)(2,1)S(1)} %get-tuple-element.51), channel_id=1, source_target_pairs={{0,12},{1,13},{2,14},{3,15},{4,0},{5,1},{6,2},{7,3},{8,4},{9,5},{1... | collective-permute-start | bytes 688136 | tf_op jit(solution)/shard_map/ppermute | solution.py:167
  47.8 6.7 %collective-permute-start.8 = (bf16[224,512]{1,0:T(8,128)(2,1)S(1)}, bf16[224,512]{1,0:T(8,128)(2,1)S(1)}, u32[]{:S(2)}, u32[]{:S(2)}) collective-permute-start(bf16[224,512]{1,0:T(8,128)(2,1)S(1)} %get-tuple-element.56), channel_id=1, source_target_pairs={{0,1},{1,2},{2,3},{3,0},{4,5},{5,6},{6,7},{7,4},{8,9},{9,10},{10,1... | collective-permute-start | bytes 688136 | tf_op jit(solution)/shard_map/ppermute | solution.py:167
  48.0 6.7 %collective-permute-start.9 = (bf16[224,512]{1,0:T(8,128)(2,1)S(1)}, bf16[224,512]{1,0:T(8,128)(2,1)S(1)}, u32[]{:S(2)}, u32[]{:S(2)}) collective-permute-start(bf16[224,512]{1,0:T(8,128)(2,1)S(1)} %get-tuple-element.59), channel_id=1, source_target_pairs={{0,3},{1,0},{2,1},{3,2},{4,7},{5,4},{6,5},{7,6},{8,11},{9,8},{10,9... | collective-permute-start | bytes 688136 | tf_op jit(solution)/shard_map/ppermute | solution.py:167
  51.2 43.4 %collective-permute-start.23 = (bf16[2,4,224,512]{3,2,1,0:T(8,128)(2,1)S(1)}, bf16[2,4,224,512]{3,2,1,0:T(8,128)(2,1)S(1)}, u32[]{:S(2)}, u32[]{:S(2)}) collective-permute-start(bf16[2,4,224,512]{3,2,1,0:T(8,128)(2,1)S(1)} %pad_maximum_fusion.1.rest_0_), channel_id=1, source_target_pairs={{0,1},{1,2},{2,3},{3,0},{4,5},{5,6},{6,7},{7,4},{8,9},{9,10},{10,1... | collective-permute-start | bytes 5505032 | tf_op jit(solution)/shard_map/ppermute | solution.py:166
  51.4 43.4 %collective-permute-start.25 = (bf16[2,4,224,512]{3,2,1,0:T(8,128)(2,1)S(1)}, bf16[2,4,224,512]{3,2,1,0:T(8,128)(2,1)S(1)}, u32[]{:S(2)}, u32[]{:S(2)}) collective-permute-start(bf16[2,4,224,512]{3,2,1,0:T(8,128)(2,1)S(1)} %pad_maximum_fusion.1.rest_0_), channel_id=1, source_target_pairs={{0,3},{1,0},{2,1},{3,2},{4,7},{5,4},{6,5},{7,6},{8,11},{9,8},{10,9... | collective-permute-start | bytes 5505032 | tf_op jit(solution)/shard_map/ppermute | solution.py:166
  55.0 43.6 %collective-permute-start.10 = (bf16[2,4,224,512]{3,2,1,0:T(8,128)(2,1)S(1)}, bf16[2,4,224,512]{3,2,1,0:T(8,128)(2,1)S(1)}, u32[]{:S(2)}, u32[]{:S(2)}) collective-permute-start(bf16[2,4,224,512]{3,2,1,0:T(8,128)(2,1)S(1)} %pad_maximum_fusion.rest_0_), channel_id=1, source_target_pairs={{0,4},{1,5},{2,6},{3,7},{4,8},{5,9},{6,10},{7,11},{8,12},{9,13},{1... | collective-permute-start | bytes 5505032 | tf_op jit(solution)/shard_map/ppermute | solution.py:166
  56.2 44.9 %collective-permute-start.12 = (bf16[2,4,224,512]{3,2,1,0:T(8,128)(2,1)S(1)}, bf16[2,4,224,512]{3,2,1,0:T(8,128)(2,1)S(1)}, u32[]{:S(2)}, u32[]{:S(2)}) collective-permute-start(bf16[2,4,224,512]{3,2,1,0:T(8,128)(2,1)S(1)} %pad_maximum_fusion.rest_0_), channel_id=1, source_target_pairs={{0,12},{1,13},{2,14},{3,15},{4,0},{5,1},{6,2},{7,3},{8,4},{9,5},{1... | collective-permute-start | bytes 5505032 | tf_op jit(solution)/shard_map/ppermute | solution.py:166
  94.6 1.6 copy-start.2
  94.6 21.2 %collective-permute-start.24 = (bf16[4,224,512]{2,1,0:T(8,128)(2,1)S(1)}, bf16[4,224,512]{2,1,0:T(8,128)(2,1)S(1)}, u32[]{:S(2)}, u32[]{:S(2)}) collective-permute-start(bf16[4,224,512]{2,1,0:T(8,128)(2,1)S(1)} %slice_bitcast_fusion.1), channel_id=1, source_target_pairs={{0,1},{1,2},{2,3},{3,0},{4,5},{5,6},{6,7},{7,4},{8,9},{9,10},{10,1... | collective-permute-start | bytes 2752520 | tf_op jit(solution)/shard_map/ppermute | solution.py:167
  94.7 5.2 %copy-start.3 = (bf16[2,4,224,512]{3,2,1,0:T(8,128)(2,1)}, bf16[2,4,224,512]{3,2,1,0:T(8,128)(2,1)S(1)}, u32[]{:S(2)}) copy-start(bf16[2,4,224,512]{3,2,1,0:T(8,128)(2,1)S(1)} %collective-permute-done.25.rest_2_) | copy-start | bytes 5505028
  96.2 20.2 %collective-permute-start.26 = (bf16[4,224,512]{2,1,0:T(8,128)(2,1)}, bf16[4,224,512]{2,1,0:T(8,128)(2,1)S(1)}, u32[]{:S(2)}, u32[]{:S(2)}) collective-permute-start(bf16[4,224,512]{2,1,0:T(8,128)(2,1)} %slice_bitcast_fusion), channel_id=1, source_target_pairs={{0,3},{1,0},{2,1},{3,2},{4,7},{5,4},{6,5},{7,6},{8,11},{9,8},{10,9... | collective-permute-start | bytes 2752520 | tf_op jit(solution)/shard_map/ppermute | solution.py:167
  98.6 1.3 copy-start.4
  99.9 35.6 %collective-permute-start.11 = (bf16[4,224,512]{2,1,0:T(8,128)(2,1)S(1)}, bf16[4,224,512]{2,1,0:T(8,128)(2,1)S(1)}, u32[]{:S(2)}, u32[]{:S(2)}) collective-permute-start(bf16[4,224,512]{2,1,0:T(8,128)(2,1)S(1)} %slice_bitcast_fusion.3), channel_id=1, source_target_pairs={{0,4},{1,5},{2,6},{3,7},{4,8},{5,9},{6,10},{7,11},{8,12},{9,13},{1... | collective-permute-start | bytes 2752520 | tf_op jit(solution)/shard_map/ppermute | solution.py:167
  101.2 1.9 %copy-start.5 = (bf16[2,4,224,512]{3,2,1,0:T(8,128)(2,1)}, bf16[2,4,224,512]{3,2,1,0:T(8,128)(2,1)S(1)}, u32[]{:S(2)}) copy-start(bf16[2,4,224,512]{3,2,1,0:T(8,128)(2,1)S(1)} %collective-permute-done.12.rest_2_) | copy-start | bytes 5505028
  101.2 34.4 %collective-permute-start.13 = (bf16[4,224,512]{2,1,0:T(8,128)(2,1)S(1)}, bf16[4,224,512]{2,1,0:T(8,128)(2,1)S(1)}, u32[]{:S(2)}, u32[]{:S(2)}) collective-permute-start(bf16[4,224,512]{2,1,0:T(8,128)(2,1)S(1)} %slice_bitcast_fusion.2), channel_id=1, source_target_pairs={{0,12},{1,13},{2,14},{3,15},{4,0},{5,1},{6,2},{7,3},{8,4},{9,5},{1... | collective-permute-start | bytes 2752520 | tf_op jit(solution)/shard_map/ppermute | solution.py:167
  120.5 23.9 %collective-permute-start.27 = (bf16[448,128]{1,0:T(8,128)(2,1)S(1)}, bf16[448,128]{1,0:T(8,128)(2,1)S(1)}, u32[]{:S(2)}, u32[]{:S(2)}) collective-permute-start(bf16[448,128]{1,0:T(8,128)(2,1)S(1)} %get-tuple-element.37), channel_id=1, source_target_pairs={{0,192},{16,208},{32,224},{48,240},{64,0},{80,16},{96,32},{112,48}... | collective-permute-start | bytes 344072 | tf_op jit(solution)/shard_map/ppermute | solution.py:215
  125.1 21.2 %collective-permute-start.28 = (bf16[448,128]{1,0:T(8,128)(2,1)S(1)}, bf16[448,128]{1,0:T(8,128)(2,1)S(1)}, u32[]{:S(2)}, u32[]{:S(2)}) collective-permute-start(bf16[448,128]{1,0:T(8,128)(2,1)S(1)} %get-tuple-element.38), channel_id=1, source_target_pairs={{0,160},{16,176},{32,192},{48,208},{64,224},{80,240},{96,0},{112,1... | collective-permute-start | bytes 344072 | tf_op jit(solution)/shard_map/ppermute | solution.py:215
  133.1 13.2 %collective-permute-start.30 = (bf16[448,128]{1,0:T(8,128)(2,1)S(1)}, bf16[448,128]{1,0:T(8,128)(2,1)S(1)}, u32[]{:S(2)}, u32[]{:S(2)}) collective-permute-start(bf16[448,128]{1,0:T(8,128)(2,1)S(1)} %get-tuple-element.40), channel_id=1, source_target_pairs={{0,96},{16,112},{32,128},{48,144},{64,160},{80,176},{96,192},{112,... | collective-permute-start | bytes 344072 | tf_op jit(solution)/shard_map/ppermute | solution.py:215
  135.5 12.6 %collective-permute-start.31 = (bf16[448,128]{1,0:T(8,128)(2,1)S(1)}, bf16[448,128]{1,0:T(8,128)(2,1)S(1)}, u32[]{:S(2)}, u32[]{:S(2)}) collective-permute-start(bf16[448,128]{1,0:T(8,128)(2,1)S(1)} %get-tuple-element.41), channel_id=1, source_target_pairs={{0,64},{16,80},{32,96},{48,112},{64,128},{80,144},{96,160},{112,17... | collective-permute-start | bytes 344072 | tf_op jit(solution)/shard_map/ppermute | solution.py:215
  139.7 8.4 %collective-permute-start.14 = (bf16[448,128]{1,0:T(8,128)(2,1)S(1)}, bf16[448,128]{1,0:T(8,128)(2,1)S(1)}, u32[]{:S(2)}, u32[]{:S(2)}) collective-permute-start(bf16[448,128]{1,0:T(8,128)(2,1)S(1)} %get-tuple-element.32), channel_id=1, source_target_pairs={{0,224},{16,240},{32,0},{48,16},{64,32},{80,48},{96,64},{112,80},{... | collective-permute-start | bytes 344072 | tf_op jit(solution)/shard_map/ppermute | solution.py:215
  144.4 9.9 %collective-permute-start.29 = (bf16[448,128]{1,0:T(8,128)(2,1)S(1)}, bf16[448,128]{1,0:T(8,128)(2,1)S(1)}, u32[]{:S(2)}, u32[]{:S(2)}) collective-permute-start(bf16[448,128]{1,0:T(8,128)(2,1)S(1)} %get-tuple-element.39), channel_id=1, source_target_pairs={{0,128},{16,144},{32,160},{48,176},{64,192},{80,208},{96,224},{112... | collective-permute-start | bytes 344072 | tf_op jit(solution)/shard_map/ppermute | solution.py:215
  146.4 10.2 %collective-permute-start.32 = (bf16[448,128]{1,0:T(8,128)(2,1)S(1)}, bf16[448,128]{1,0:T(8,128)(2,1)S(1)}, u32[]{:S(2)}, u32[]{:S(2)}) collective-permute-start(bf16[448,128]{1,0:T(8,128)(2,1)S(1)} %get-tuple-element.42), channel_id=1, source_target_pairs={{0,32},{16,48},{32,64},{48,80},{64,96},{80,112},{96,128},{112,144}... | collective-permute-start | bytes 344072 | tf_op jit(solution)/shard_map/ppermute | solution.py:215
  157.8 4.7 %collective-permute-start.33 = (f32[128,448]{1,0:T(8,128)S(1)}, f32[128,448]{1,0:T(8,128)S(1)}, u32[]{:S(2)}, u32[]{:S(2)}) collective-permute-start(f32[128,448]{1,0:T(8,128)S(1)} %get-tuple-element.44), channel_id=1, source_target_pairs={{0,16},{16,0},{32,48},{48,32},{64,80},{80,64},{96,112},{112,96},{1... | collective-permute-start | bytes 688136 | tf_op jit(solution)/shard_map/ppermute | solution.py:205

commit v2 on v1

--- a/solution.py
+++ b/solution.py
@@ -119,16 +119,22 @@
                 copies.append(pltpu.make_async_copy(source, target, sems.at[len(copies)]))
                 copies[-1].start()
     count = len(copies) // held.shape[0]
-    for g in range(held.shape[0]):
-        for copy in copies[g * count : (g + 1) * count]:
+    if early:
+        for g in range(held.shape[0]):
+            for copy in copies[g * count : (g + 1) * count]:
+                copy.wait()
+            total = dot(held[g], gathered[g])
+            outs[0][...] = total if g == 0 else total + outs[0][...]
+        return
+    total = before[0][...]
+    for first in range(SIDE):
+        for copy in copies[first * 3 : first * 3 + 3]:
             copy.wait()
-        total = dot(held[g], gathered[g])
-        if early:
-            outs[0][...] = total if g == 0 else total + outs[0][...]
-    if not early:
-        total = (total + before[0][...]).astype(jnp.bfloat16)
-        for b, block in enumerate(outs):
-            block[...] = total[:, b * WIDE : (b + 1) * WIDE]
+        span = pl.ds(first * WINDOW, WINDOW)
+        total += dot(held[0, :, span], gathered[0, span, :])
+    total = total.astype(jnp.bfloat16)
+    for b, block in enumerate(outs):
+        block[...] = total[:, b * WIDE : (b + 1) * WIDE]
 
 
 def times_ring(factor, x_first, pieces, before=()):
@@ -167,15 +173,15 @@
     return behind, ahead, lax.ppermute(behind[0], "panel", way(1)), lax.ppermute(ahead[1], "panel", way(-1))
 
 
-def ring_product(factor, block, x_first):
+def ring_gather(blocks, x_first):
+    block = jnp.concatenate(blocks, 1)
     feat, width = block.shape
     ways = (along_x, along_y) if x_first else (along_y, along_x)
     mine = block.reshape(2, feat // 2, width)
     behind, ahead, *across = go_round(mine, ways[0])
     line = jnp.stack([jnp.stack([mine[j], behind[j], ahead[j], across[j]]) for j in range(2)])
     behind, ahead, *across = go_round(line, ways[1])
-    early = times_ring(factor, x_first, [line, behind, ahead])
-    return times_ring(factor, x_first, across, early)
+    return [line, behind, ahead], across
 
 
 def combine_kernel(count, high, low, *rest):
@@ -205,14 +211,22 @@
     swap = lambda a: lax.ppermute(a, "expert", SWAP)
     mine = expert_ids.T, mix_weights.T, jnp.transpose(queries, (1, 0, 2))
     blocks, high, low = route(mine, tuple(map(swap, mine)))
-    arrived = {k: lax.ppermute(blocks[k], "expert", along_z(k)) if k else blocks[k] for k in range(CHIPS)}
-
-    product = {}
-    for shifts in (X_FIRST, Y_FIRST):
-        block = jnp.concatenate([arrived[k] for k in shifts], 1)
-        product |= dict(zip(shifts, ring_product(factors[0], block, shifts is X_FIRST)))
-
-    returned = [lax.ppermute(product[k], "expert", along_z(-k)) if k else product[k] for k in range(CHIPS)]
+    after = lax.optimization_barrier
+    send = lambda k, a: lax.ppermute(a, "expert", along_z(k)) if k % CHIPS else a
+    first = [send(k, blocks[k]) for k in X_FIRST]
+    second = [send(k, blocks[k]) for k in Y_FIRST]
+
+    factor = factors[0]
+    near_x, far_x = ring_gather(first, True)
+    near_y, far_y = ring_gather(second, False)
+    early_x = times_ring(factor, True, near_x)
+    early_y = times_ring(factor, False, near_y)
+    far_x, early_y = after((far_x, early_y))
+    late_x = times_ring(factor, True, far_x, early_x)
+    late_y = times_ring(factor, False, far_y, early_y)
+
+    returned = {k: send(-k, block) for k, block in zip(X_FIRST + Y_FIRST, late_x + late_y)}
+    returned = [returned[k] for k in range(CHIPS)]
     own, other = combine(high, low, returned)
     return (own + swap(other)).astype(jnp.bfloat16)
 

time: 164 us -> 159 us (0.970)
  waiting for transfers between devices: 68.1 us -> 59.2 us
  starting transfers between devices: 61.1 us -> 65.6 us
    ppermute x8, waiting for transfers between devices: 43.4 us -> 37.5 us  [go_round(): behind, ahead = (lax.ppermute(parts, 'panel', way(by)) for by in (1, -1))]
    ppermute x4, waiting for transfers between devices: 6.33 us -> 3.14 us  [go_round(): lax.ppermute(behind[0], 'panel', way(1))]
    ppermute x14, starting transfers between devices: 31 us -> 33.3 us  [on_device(): lax.ppermute(a, 'expert', along_z(k))]
    ppermute x4, starting transfers between devices: 7.37 us -> 9.34 us  [on_device(): swap = lambda a: lax.ppermute(a, 'expert', SWAP)]
    ppermute x4, starting transfers between devices: 9.73 us -> 11.4 us  [go_round(): lax.ppermute(ahead[1], 'panel', way(-1))]
  transfers between devices with their start and end apart: 34 -> 34, of which waited for: 15 -> 11; matrix products, arithmetic and copies ran while one was open for 2% -> 2% of each run, Pallas kernels for 14% -> 14%
where the time goes in v2:
time: 159 us
  starting transfers between devices  65.6 us (41%)
  waiting for transfers between devices  59.2 us (37%)
  Pallas kernels  25.8 us (16%)
  local copies, waits for them, and re-layouts  7.24 us (5%)
    ppermute x8, waiting for transfers between devices, go_round(): behind, ahead = (lax.ppermute(parts, 'panel', way(by)) for by in (1, -1))  37.5 us
    ppermute x14, starting transfers between devices, on_device(): lax.ppermute(a, 'expert', along_z(k))  33.3 us
    pallas_call x4, Pallas kernels, times_ring(): pl.pallas_call(functools.partial(ring_kernel, x_first, early), in_specs=[...  21.8 us
    ppermute x14, waiting for transfers between devices, on_device(): lax.ppermute(a, 'expert', along_z(k))  14.7 us
    ppermute x4, starting transfers between devices, go_round(): lax.ppermute(ahead[1], 'panel', way(-1))  11.4 us
    ppermute x8, starting transfers between devices, go_round(): behind, ahead = (lax.ppermute(parts, 'panel', way(by)) for by in (1, -1))  9.84 us
    ppermute x4, starting transfers between devices, on_device(): swap = lambda a: lax.ppermute(a, 'expert', SWAP)  9.34 us
    unnamed x19, local copies, waits for them, and re-layouts  4.83 us
  transfers between devices with their start and end apart: 34, of which 11 were waited for; matrix products, arithmetic and copies ran while one was open for 2% of the time, Pallas kernels for 14%

profile of v2, /device:TPU:1, one launch (start us, length us, event | category | flops | bytes accessed | tf_op | source)
XLA Modules:
  0.0 159.1 jit_solution(15840858509267099235)
XLA Ops:
  0.0 1.2 copy.5
  1.2 3.3 %collective-permute-start.2 = (bf16[4,128,448]{2,1,0:T(8,128)(2,1)S(1)}, bf16[4,128,448]{2,1,0:T(8,128)(2,1)S(1)}, u32[]{:S(2)}, u32[]{:S(2)}) collective-permute-start(bf16[4,128,448]{2,1,0:T(8,128)(2,1)S(1)} %bitcast.42), channel_id=1, source_target_pairs={{0,16},{16,0},{32,48},{48,32},{64,80},{80,64},{96,112},{112,96},{1... | collective-permute-start | bytes 1376264 | tf_op jit(solution)/shard_map/ppermute | solution.py:211
  4.6 0.1 collective-permute-start
  4.7 0.4 collective-permute-start.1
  5.1 1.2 collective-permute-done.other_ids
  6.3 0.7 copy-done
  7.0 0.7 copy-done.1
  7.7 2.8 %route.1 = (bf16[448,128]{1,0:T(8,128)(2,1)S(1)}, bf16[448,128]{1,0:T(8,128)(2,1)S(1)}, bf16[448,128]{1,0:T(8,128)(2,1)S(1)}, bf16[448,128]{1,0:T(8,128)(2,1)S(1...) custom-call(s32[4,128]{1,0:T(4,128)S(1)} %bitcast.45, ...), custom_call_target="tpu_custom_call" | custom-call | tf_op jit(solution)/shard_map/route/pallas_call | solution.py:83
  10.5 0.1 collective-permute-start.3
  10.6 3.9 %collective-permute-start.4 = (bf16[448,128]{1,0:T(8,128)(2,1)S(1)}, bf16[448,128]{1,0:T(8,128)(2,1)S(1)}, u32[]{:S(2)}, u32[]{:S(2)}) collective-permute-start(bf16[448,128]{1,0:T(8,128)(2,1)S(1)} %get-tuple-element.32), channel_id=1, source_target_pairs={{0,224},{16,240},{32,0},{48,16},{64,32},{80,48},{96,64},{112,80},{... | collective-permute-start | bytes 344072 | tf_op jit(solution)/shard_map/ppermute | solution.py:215
  14.5 3.9 %collective-permute-start.5 = (bf16[448,128]{1,0:T(8,128)(2,1)S(1)}, bf16[448,128]{1,0:T(8,128)(2,1)S(1)}, u32[]{:S(2)}, u32[]{:S(2)}) collective-permute-start(bf16[448,128]{1,0:T(8,128)(2,1)S(1)} %get-tuple-element.33), channel_id=1, source_target_pairs={{0,128},{16,144},{32,160},{48,176},{64,192},{80,208},{96,224},{112... | collective-permute-start | bytes 344072 | tf_op jit(solution)/shard_map/ppermute | solution.py:215
  18.4 3.6 %collective-permute-start.15 = (bf16[448,128]{1,0:T(8,128)(2,1)S(1)}, bf16[448,128]{1,0:T(8,128)(2,1)S(1)}, u32[]{:S(2)}, u32[]{:S(2)}) collective-permute-start(bf16[448,128]{1,0:T(8,128)(2,1)S(1)} %get-tuple-element.35), channel_id=1, source_target_pairs={{0,192},{16,208},{32,224},{48,240},{64,0},{80,16},{96,32},{112,48}... | collective-permute-start | bytes 344072 | tf_op jit(solution)/shard_map/ppermute | solution.py:215
  22.0 0.1 collective-permute-start.16
  22.1 4.5 %collective-permute-start.17 = (bf16[448,128]{1,0:T(8,128)(2,1)S(1)}, bf16[448,128]{1,0:T(8,128)(2,1)S(1)}, u32[]{:S(2)}, u32[]{:S(2)}) collective-permute-start(bf16[448,128]{1,0:T(8,128)(2,1)S(1)} %get-tuple-element.37), channel_id=1, source_target_pairs={{0,160},{16,176},{32,192},{48,208},{64,224},{80,240},{96,0},{112,1... | collective-permute-start | bytes 344072 | tf_op jit(solution)/shard_map/ppermute | solution.py:215
  26.8 2.8 %collective-permute-start.7 = (bf16[2,224,512]{2,1,0:T(8,128)(2,1)S(1)}, bf16[2,224,512]{2,1,0:T(8,128)(2,1)S(1)}, u32[]{:S(2)}, u32[]{:S(2)}) collective-permute-start(bf16[2,224,512]{2,1,0:T(8,128)(2,1)S(1)} %bitcast.52), channel_id=1, source_target_pairs={{0,3},{1,0},{2,1},{3,2},{4,7},{5,4},{6,5},{7,6},{8,11},{9,8},{10,9... | collective-permute-start | bytes 1376264 | tf_op jit(solution)/shard_map/ppermute | solution.py:172
  29.6 1.5 collective-permute-done.15
  31.1 5.0 %collective-permute-done.16 = bf16[448,128]{1,0:T(8,128)(2,1)S(1)} collective-permute-done((bf16[448,128]{1,0:T(8,128)(2,1)S(1)}, bf16[448,128]{1,0:T(8,128)(2,1)S(1)}, u32[]{:S(2)}, u32[]{:S(2)}) %collective-permute-start.16) | collective-permute-done | bytes 114720 | tf_op jit(solution)/shard_map/ppermute | solution.py:215
  36.2 2.6 %collective-permute-start.19 = (bf16[2,224,512]{2,1,0:T(8,128)(2,1)S(1)}, bf16[2,224,512]{2,1,0:T(8,128)(2,1)S(1)}, u32[]{:S(2)}, u32[]{:S(2)}) collective-permute-start(bf16[2,224,512]{2,1,0:T(8,128)(2,1)S(1)} %bitcast.54), channel_id=1, source_target_pairs={{0,12},{1,13},{2,14},{3,15},{4,0},{5,1},{6,2},{7,3},{8,4},{9,5},{1... | collective-permute-start | bytes 1376264 | tf_op jit(solution)/shard_map/ppermute | solution.py:172
  38.8 0.1 fusion.3
  38.8 2.8 %collective-permute-start.9 = (bf16[224,512]{1,0:T(8,128)(2,1)S(1)}, bf16[224,512]{1,0:T(8,128)(2,1)S(1)}, u32[]{:S(2)}, u32[]{:S(2)}) collective-permute-start(bf16[224,512]{1,0:T(8,128)(2,1)S(1)} %get-tuple-element.65), channel_id=1, source_target_pairs={{0,3},{1,0},{2,1},{3,2},{4,7},{5,4},{6,5},{7,6},{8,11},{9,8},{10,9... | collective-permute-start | bytes 688136 | tf_op jit(solution)/shard_map/ppermute | solution.py:173
  41.7 4.8 %collective-permute-done.19 = bf16[2,224,512]{2,1,0:T(8,128)(2,1)S(1)} collective-permute-done((bf16[2,224,512]{2,1,0:T(8,128)(2,1)S(1)}, bf16[2,224,512]{2,1,0:T(8,128)(2,1)S(1)}, u32[]{:S(2)}, u32[]{:S(2)}) %collective-permute-start.19) | collective-permute-done | bytes 458784 | tf_op jit(solution)/shard_map/ppermute | solution.py:172
  46.5 3.5 %collective-permute-start.21 = (bf16[224,512]{1,0:T(8,128)(2,1)S(1)}, bf16[224,512]{1,0:T(8,128)(2,1)S(1)}, u32[]{:S(2)}, u32[]{:S(2)}) collective-permute-start(bf16[224,512]{1,0:T(8,128)(2,1)S(1)} %get-tuple-element.57), channel_id=1, source_target_pairs={{0,12},{1,13},{2,14},{3,15},{4,0},{5,1},{6,2},{7,3},{8,4},{9,5},{1... | collective-permute-start | bytes 688136 | tf_op jit(solution)/shard_map/ppermute | solution.py:173
  50.0 0.1 collective-permute-start.20
  50.1 0.1 fusion.2
  50.2 1.3 collective-permute-start.8
  51.5 1.4 collective-permute-done.21
  52.9 0.1 maximum_bitcast_fusion.3
  53.0 3.1 %collective-permute-done.20 = bf16[224,512]{1,0:T(8,128)(2,1)S(1)} collective-permute-done((bf16[224,512]{1,0:T(8,128)(2,1)S(1)}, bf16[224,512]{1,0:T(8,128)(2,1)S(1)}, u32[]{:S(2)}, u32[]{:S(2)}) %collective-permute-start.20) | collective-permute-done | bytes 229408 | tf_op jit(solution)/shard_map/ppermute | solution.py:173
  56.2 0.1 maximum_bitcast_fusion.2
  56.3 0.2 pad_maximum_fusion.1.rest_0_
  56.5 2.9 %collective-permute-start.24 = (bf16[2,4,224,512]{3,2,1,0:T(8,128)(2,1)S(1)}, bf16[2,4,224,512]{3,2,1,0:T(8,128)(2,1)S(1)}, u32[]{:S(2)}, u32[]{:S(2)}) collective-permute-start(bf16[2,4,224,512]{3,2,1,0:T(8,128)(2,1)S(1)} %pad_maximum_fusion.1.rest_0_), channel_id=1, source_target_pairs={{0,3},{1,0},{2,1},{3,2},{4,7},{5,4},{6,5},{7,6},{8,11},{9,8},{10,9... | collective-permute-start | bytes 5505032 | tf_op jit(solution)/shard_map/ppermute | solution.py:172
  59.4 0.1 collective-permute-start.22
  59.5 0.1 maximum_bitcast_fusion.1
  59.6 0.1 maximum_bitcast_fusion
  59.7 0.2 pad_maximum_fusion.rest_0_
  59.9 0.1 collective-permute-start.12
  60.0 1.5 collective-permute-start.10
  61.5 32.7 %collective-permute-done.24.rest_2_ = bf16[2,4,224,512]{3,2,1,0:T(8,128)(2,1)S(1)} collective-permute-done((bf16[2,4,224,512]{3,2,1,0:T(8,128)(2,1)S(1)}, bf16[2,4,224,512]{3,2,1,0:T(8,128)(2,1)S(1)}, u32[]{:S(2)}, u32[]{:S(2)}) %collective-permute-start.24) | collective-permute-done | bytes 1835040 | tf_op jit(solution)/shard_map/ppermute | solution.py:172
  94.2 0.1 slice_bitcast_fusion
  94.3 3.5 %collective-permute-start.25 = (bf16[4,224,512]{2,1,0:T(8,128)(2,1)S(1)}, bf16[4,224,512]{2,1,0:T(8,128)(2,1)S(1)}, u32[]{:S(2)}, u32[]{:S(2)}) collective-permute-start(bf16[4,224,512]{2,1,0:T(8,128)(2,1)S(1)} %slice_bitcast_fusion), channel_id=1, source_target_pairs={{0,3},{1,0},{2,1},{3,2},{4,7},{5,4},{6,5},{7,6},{8,11},{9,8},{10,9... | collective-permute-start | bytes 2752520 | tf_op jit(solution)/shard_map/ppermute | solution.py:173
  97.8 1.1 slice_bitcast_fusion.1
  98.9 1.2 copy-done.4
  100.1 0.1 slice_bitcast_fusion.2
  100.2 1.6 %collective-permute-start.13 = (bf16[4,224,512]{2,1,0:T(8,128)(2,1)S(1)}, bf16[4,224,512]{2,1,0:T(8,128)(2,1)S(1)}, u32[]{:S(2)}, u32[]{:S(2)}) collective-permute-start(bf16[4,224,512]{2,1,0:T(8,128)(2,1)S(1)} %slice_bitcast_fusion.2), channel_id=1, source_target_pairs={{0,12},{1,13},{2,14},{3,15},{4,0},{5,1},{6,2},{7,3},{8,4},{9,5},{1... | collective-permute-start | bytes 2752520 | tf_op jit(solution)/shard_map/ppermute | solution.py:173
  101.8 0.1 slice_bitcast_fusion.3
  101.9 0.3 collective-permute-start.11
  102.2 0.9 copy-done.5
  103.1 7.0 %times_ring_early.3.rest_2_ = f32[448,512]{1,0:T(8,128)S(1)} custom-call(bf16[448,7168]{1,0:T(8,128)(2,1)} %bitcast.48, bf16[2,4,224,512]{3,2,1,0:T(8,128)(2,1)S(1)} %pad_maximum_fusion.1.rest_0_, bf16[2,4,224,512]{3,2,1,0:T(8,128)(2,1)} %copy-done.3, bf16[2,4,224,512]{3,2,1,0:T(8,128)(2,1)} %copy-done.2), custom_call_target="tpu_custom_call" | custom-call | flops 2818572288 | bytes 11796480 | tf_op jit(solution)/shard_map/times_ring_early/pallas_call | solution.py:151
  110.1 7.0 %times_ring_early.2.rest_2_ = f32[448,512]{1,0:T(8,128)S(1)} custom-call(bf16[448,7168]{1,0:T(8,128)(2,1)} %bitcast.49, bf16[2,4,224,512]{3,2,1,0:T(8,128)(2,1)S(1)} %pad_maximum_fusion.rest_0_, bf16[2,4,224,512]{3,2,1,0:T(8,128)(2,1)} %copy-done.5, bf16[2,4,224,512]{3,2,1,0:T(8,128)(2,1)} %copy-done.4), custom_call_target="tpu_custom_call" | custom-call | flops 2818572288 | bytes 11796480 | tf_op jit(solution)/shard_map/times_ring_early/pallas_call | solution.py:151
  117.1 3.9 %times_ring_late.3 = (bf16[448,128]{1,0:T(8,128)(2,1)S(1)}, bf16[448,128]{1,0:T(8,128)(2,1)S(1)}, bf16[448,128]{1,0:T(8,128)(2,1)S(1)}, bf16[448,128]{1,0:T(8,128)(2,1)S(1)}) custom-call(bf16[448,7168]{1,0:T(8,128)(2,1)} %bitcast.50, bf16[4,224,512]{2,1,0:T(8,128)(2,1)S(1)} %collective-permute-done.23.rest_0_, ...), custom_call_target="tpu_custom_call" | custom-call | flops 939524096 | bytes 3932160 | tf_op jit(solution)/shard_map/times_ring_late/pallas_call | solution.py:151
  121.0 6.7 %collective-permute-start.27 = (bf16[448,128]{1,0:T(8,128)(2,1)S(1)}, bf16[448,128]{1,0:T(8,128)(2,1)S(1)}, u32[]{:S(2)}, u32[]{:S(2)}) collective-permute-start(bf16[448,128]{1,0:T(8,128)(2,1)S(1)} %get-tuple-element.43), channel_id=1, source_target_pairs={{0,192},{16,208},{32,224},{48,240},{64,0},{80,16},{96,32},{112,48}... | collective-permute-start | bytes 344072 | tf_op jit(solution)/shard_map/ppermute | solution.py:215
  127.8 1.6 %collective-permute-start.28 = (bf16[448,128]{1,0:T(8,128)(2,1)S(1)}, bf16[448,128]{1,0:T(8,128)(2,1)S(1)}, u32[]{:S(2)}, u32[]{:S(2)}) collective-permute-start(bf16[448,128]{1,0:T(8,128)(2,1)S(1)} %get-tuple-element.44), channel_id=1, source_target_pairs={{0,160},{16,176},{32,192},{48,208},{64,224},{80,240},{96,0},{112,1... | collective-permute-start | bytes 344072 | tf_op jit(solution)/shard_map/ppermute | solution.py:215
  129.4 1.6 %collective-permute-start.30 = (bf16[448,128]{1,0:T(8,128)(2,1)S(1)}, bf16[448,128]{1,0:T(8,128)(2,1)S(1)}, u32[]{:S(2)}, u32[]{:S(2)}) collective-permute-start(bf16[448,128]{1,0:T(8,128)(2,1)S(1)} %get-tuple-element.46), channel_id=1, source_target_pairs={{0,96},{16,112},{32,128},{48,144},{64,160},{80,176},{96,192},{112,... | collective-permute-start | bytes 344072 | tf_op jit(solution)/shard_map/ppermute | solution.py:215
  131.0 3.9 %times_ring_late.2 = (bf16[448,128]{1,0:T(8,128)(2,1)S(1)}, bf16[448,128]{1,0:T(8,128)(2,1)S(1)}, bf16[448,128]{1,0:T(8,128)(2,1)S(1)}, bf16[448,128]{1,0:T(8,128)(2,1)S(1)}) custom-call(bf16[448,7168]{1,0:T(8,128)(2,1)} %bitcast.51, bf16[4,224,512]{2,1,0:T(8,128)(2,1)S(1)} %collective-permute-done.11.rest_0_, ...), custom_call_target="tpu_custom_call" | custom-call | flops 939524096 | bytes 3932160 | tf_op jit(solution)/shard_map/times_ring_late/pallas_call | solution.py:151
  134.9 5.0 %collective-permute-start.26 = (bf16[448,128]{1,0:T(8,128)(2,1)S(1)}, bf16[448,128]{1,0:T(8,128)(2,1)S(1)}, u32[]{:S(2)}, u32[]{:S(2)}) collective-permute-start(bf16[448,128]{1,0:T(8,128)(2,1)S(1)} %get-tuple-element.40), channel_id=1, source_target_pairs={{0,224},{16,240},{32,0},{48,16},{64,32},{80,48},{96,64},{112,80},{... | collective-permute-start | bytes 344072 | tf_op jit(solution)/shard_map/ppermute | solution.py:215
  139.9 1.5 collective-permute-start.29
  141.4 0.7 collective-permute-start.32
  142.1 1.6 collective-permute-done.26.rest_1_
  143.7 5.9 %collective-permute-done.29.rest_4_ = bf16[448,128]{1,0:T(8,128)(2,1)S(1)} collective-permute-done((bf16[448,128]{1,0:T(8,128)(2,1)S(1)}, bf16[448,128]{1,0:T(8,128)(2,1)S(1)}, u32[]{:S(2)}, u32[]{:S(2)}) %collective-permute-start.29) | collective-permute-done | bytes 114720 | tf_op jit(solution)/shard_map/ppermute | solution.py:215
  149.6 0.8 collective-permute-done.32.rest_7_
  150.4 1.2 combine.1
  151.6 5.5 %collective-permute-start.33 = (f32[128,448]{1,0:T(8,128)S(1)}, f32[128,448]{1,0:T(8,128)S(1)}, u32[]{:S(2)}, u32[]{:S(2)}) collective-permute-start(f32[128,448]{1,0:T(8,128)S(1)} %get-tuple-element.50), channel_id=1, source_target_pairs={{0,16},{16,0},{32,48},{48,32},{64,80},{80,64},{96,112},{112,96},{1... | collective-permute-start | bytes 688136 | tf_op jit(solution)/shard_map/ppermute | solution.py:211
  157.1 1.2 collective-permute-done.33
  158.3 0.8 copy.6
  (49 shorter events, 0.5 us)
Async XLA Ops:
  1.2 5.1 %collective-permute-start.2 = (bf16[4,128,448]{2,1,0:T(8,128)(2,1)S(1)}, bf16[4,128,448]{2,1,0:T(8,128)(2,1)S(1)}, u32[]{:S(2)}, u32[]{:S(2)}) collective-permute-start(bf16[4,128,448]{2,1,0:T(8,128)(2,1)S(1)} %bitcast.42), channel_id=1, source_target_pairs={{0,16},{16,0},{32,48},{48,32},{64,80},{80,64},{96,112},{112,96},{1... | collective-permute-start | bytes 1376264 | tf_op jit(solution)/shard_map/ppermute | solution.py:211
  4.6 1.8 %collective-permute-start = (s32[4,128]{1,0:T(4,128)}, s32[4,128]{1,0:T(4,128)S(1)}, u32[]{:S(2)}, u32[]{:S(2)}) collective-permute-start(s32[4,128]{1,0:T(4,128)} %bitcast.44), channel_id=1, source_target_pairs={{0,16},{16,0},{32,48},{48,32},{64,80},{80,64},{96,112},{112,96},{1... | collective-permute-start | bytes 6152 | tf_op jit(solution)/shard_map/ppermute | solution.py:211
  4.7 1.7 %collective-permute-start.1 = (f32[4,128]{1,0:T(4,128)}, f32[4,128]{1,0:T(4,128)S(1)}, u32[]{:S(2)}, u32[]{:S(2)}) collective-permute-start(f32[4,128]{1,0:T(4,128)} %bitcast.46), channel_id=1, source_target_pairs={{0,16},{16,0},{32,48},{48,32},{64,80},{80,64},{96,112},{112,96},{1... | collective-permute-start | bytes 6152 | tf_op jit(solution)/shard_map/ppermute | solution.py:211
  6.3 0.7 copy-start
  7.0 0.7 copy-start.1
  10.5 11.5 %collective-permute-start.3 = (bf16[448,128]{1,0:T(8,128)(2,1)S(1)}, bf16[448,128]{1,0:T(8,128)(2,1)S(1)}, u32[]{:S(2)}, u32[]{:S(2)}) collective-permute-start(bf16[448,128]{1,0:T(8,128)(2,1)S(1)} %get-tuple-element.31), channel_id=1, source_target_pairs={{0,32},{16,48},{32,64},{48,80},{64,96},{80,112},{96,128},{112,144}... | collective-permute-start | bytes 344072 | tf_op jit(solution)/shard_map/ppermute | solution.py:215
  10.6 11.6 %collective-permute-start.4 = (bf16[448,128]{1,0:T(8,128)(2,1)S(1)}, bf16[448,128]{1,0:T(8,128)(2,1)S(1)}, u32[]{:S(2)}, u32[]{:S(2)}) collective-permute-start(bf16[448,128]{1,0:T(8,128)(2,1)S(1)} %get-tuple-element.32), channel_id=1, source_target_pairs={{0,224},{16,240},{32,0},{48,16},{64,32},{80,48},{96,64},{112,80},{... | collective-permute-start | bytes 344072 | tf_op jit(solution)/shard_map/ppermute | solution.py:215
  14.5 12.2 %collective-permute-start.5 = (bf16[448,128]{1,0:T(8,128)(2,1)S(1)}, bf16[448,128]{1,0:T(8,128)(2,1)S(1)}, u32[]{:S(2)}, u32[]{:S(2)}) collective-permute-start(bf16[448,128]{1,0:T(8,128)(2,1)S(1)} %get-tuple-element.33), channel_id=1, source_target_pairs={{0,128},{16,144},{32,160},{48,176},{64,192},{80,208},{96,224},{112... | collective-permute-start | bytes 344072 | tf_op jit(solution)/shard_map/ppermute | solution.py:215
  18.4 11.2 %collective-permute-start.14 = (bf16[448,128]{1,0:T(8,128)(2,1)S(1)}, bf16[448,128]{1,0:T(8,128)(2,1)S(1)}, u32[]{:S(2)}, u32[]{:S(2)}) collective-permute-start(bf16[448,128]{1,0:T(8,128)(2,1)S(1)} %get-tuple-element.34), channel_id=1, source_target_pairs={{0,64},{16,80},{32,96},{48,112},{64,128},{80,144},{96,160},{112,17... | collective-permute-start | bytes 344072 | tf_op jit(solution)/shard_map/ppermute | solution.py:215
  18.4 12.7 %collective-permute-start.15 = (bf16[448,128]{1,0:T(8,128)(2,1)S(1)}, bf16[448,128]{1,0:T(8,128)(2,1)S(1)}, u32[]{:S(2)}, u32[]{:S(2)}) collective-permute-start(bf16[448,128]{1,0:T(8,128)(2,1)S(1)} %get-tuple-element.35), channel_id=1, source_target_pairs={{0,192},{16,208},{32,224},{48,240},{64,0},{80,16},{96,32},{112,48}... | collective-permute-start | bytes 344072 | tf_op jit(solution)/shard_map/ppermute | solution.py:215
  22.0 14.1 %collective-permute-start.16 = (bf16[448,128]{1,0:T(8,128)(2,1)S(1)}, bf16[448,128]{1,0:T(8,128)(2,1)S(1)}, u32[]{:S(2)}, u32[]{:S(2)}) collective-permute-start(bf16[448,128]{1,0:T(8,128)(2,1)S(1)} %get-tuple-element.36), channel_id=1, source_target_pairs={{0,96},{16,112},{32,128},{48,144},{64,160},{80,176},{96,192},{112,... | collective-permute-start | bytes 344072 | tf_op jit(solution)/shard_map/ppermute | solution.py:215
  22.1 14.0 %collective-permute-start.17 = (bf16[448,128]{1,0:T(8,128)(2,1)S(1)}, bf16[448,128]{1,0:T(8,128)(2,1)S(1)}, u32[]{:S(2)}, u32[]{:S(2)}) collective-permute-start(bf16[448,128]{1,0:T(8,128)(2,1)S(1)} %get-tuple-element.37), channel_id=1, source_target_pairs={{0,160},{16,176},{32,192},{48,208},{64,224},{80,240},{96,0},{112,1... | collective-permute-start | bytes 344072 | tf_op jit(solution)/shard_map/ppermute | solution.py:215
  26.8 12.0 %collective-permute-start.7 = (bf16[2,224,512]{2,1,0:T(8,128)(2,1)S(1)}, bf16[2,224,512]{2,1,0:T(8,128)(2,1)S(1)}, u32[]{:S(2)}, u32[]{:S(2)}) collective-permute-start(bf16[2,224,512]{2,1,0:T(8,128)(2,1)S(1)} %bitcast.52), channel_id=1, source_target_pairs={{0,3},{1,0},{2,1},{3,2},{4,7},{5,4},{6,5},{7,6},{8,11},{9,8},{10,9... | collective-permute-start | bytes 1376264 | tf_op jit(solution)/shard_map/ppermute | solution.py:172
  29.6 20.6 %collective-permute-start.6 = (bf16[2,224,512]{2,1,0:T(8,128)(2,1)S(1)}, bf16[2,224,512]{2,1,0:T(8,128)(2,1)S(1)}, u32[]{:S(2)}, u32[]{:S(2)}) collective-permute-start(bf16[2,224,512]{2,1,0:T(8,128)(2,1)S(1)} %bitcast.53), channel_id=1, source_target_pairs={{0,1},{1,2},{2,3},{3,0},{4,5},{5,6},{6,7},{7,4},{8,9},{9,10},{10,1... | collective-permute-start | bytes 1376264 | tf_op jit(solution)/shard_map/ppermute | solution.py:172
  36.2 10.3 %collective-permute-start.19 = (bf16[2,224,512]{2,1,0:T(8,128)(2,1)S(1)}, bf16[2,224,512]{2,1,0:T(8,128)(2,1)S(1)}, u32[]{:S(2)}, u32[]{:S(2)}) collective-permute-start(bf16[2,224,512]{2,1,0:T(8,128)(2,1)S(1)} %bitcast.54), channel_id=1, source_target_pairs={{0,12},{1,13},{2,14},{3,15},{4,0},{5,1},{6,2},{7,3},{8,4},{9,5},{1... | collective-permute-start | bytes 1376264 | tf_op jit(solution)/shard_map/ppermute | solution.py:172
  38.7 11.2 %collective-permute-start.18 = (bf16[2,224,512]{2,1,0:T(8,128)(2,1)S(1)}, bf16[2,224,512]{2,1,0:T(8,128)(2,1)S(1)}, u32[]{:S(2)}, u32[]{:S(2)}) collective-permute-start(bf16[2,224,512]{2,1,0:T(8,128)(2,1)S(1)} %bitcast.55), channel_id=1, source_target_pairs={{0,4},{1,5},{2,6},{3,7},{4,8},{5,9},{6,10},{7,11},{8,12},{9,13},{1... | collective-permute-start | bytes 1376264 | tf_op jit(solution)/shard_map/ppermute | solution.py:172
  38.8 20.6 %collective-permute-start.9 = (bf16[224,512]{1,0:T(8,128)(2,1)S(1)}, bf16[224,512]{1,0:T(8,128)(2,1)S(1)}, u32[]{:S(2)}, u32[]{:S(2)}) collective-permute-start(bf16[224,512]{1,0:T(8,128)(2,1)S(1)} %get-tuple-element.65), channel_id=1, source_target_pairs={{0,3},{1,0},{2,1},{3,2},{4,7},{5,4},{6,5},{7,6},{8,11},{9,8},{10,9... | collective-permute-start | bytes 688136 | tf_op jit(solution)/shard_map/ppermute | solution.py:173
  46.5 6.5 %collective-permute-start.21 = (bf16[224,512]{1,0:T(8,128)(2,1)S(1)}, bf16[224,512]{1,0:T(8,128)(2,1)S(1)}, u32[]{:S(2)}, u32[]{:S(2)}) collective-permute-start(bf16[224,512]{1,0:T(8,128)(2,1)S(1)} %get-tuple-element.57), channel_id=1, source_target_pairs={{0,12},{1,13},{2,14},{3,15},{4,0},{5,1},{6,2},{7,3},{8,4},{9,5},{1... | collective-permute-start | bytes 688136 | tf_op jit(solution)/shard_map/ppermute | solution.py:173
  50.0 6.2 %collective-permute-start.20 = (bf16[224,512]{1,0:T(8,128)(2,1)S(1)}, bf16[224,512]{1,0:T(8,128)(2,1)S(1)}, u32[]{:S(2)}, u32[]{:S(2)}) collective-permute-start(bf16[224,512]{1,0:T(8,128)(2,1)S(1)} %get-tuple-element.54), channel_id=1, source_target_pairs={{0,4},{1,5},{2,6},{3,7},{4,8},{5,9},{6,10},{7,11},{8,12},{9,13},{1... | collective-permute-start | bytes 688136 | tf_op jit(solution)/shard_map/ppermute | solution.py:173
  50.2 9.4 %collective-permute-start.8 = (bf16[224,512]{1,0:T(8,128)(2,1)S(1)}, bf16[224,512]{1,0:T(8,128)(2,1)S(1)}, u32[]{:S(2)}, u32[]{:S(2)}) collective-permute-start(bf16[224,512]{1,0:T(8,128)(2,1)S(1)} %get-tuple-element.62), channel_id=1, source_target_pairs={{0,1},{1,2},{2,3},{3,0},{4,5},{5,6},{6,7},{7,4},{8,9},{9,10},{10,1... | collective-permute-start | bytes 688136 | tf_op jit(solution)/shard_map/ppermute | solution.py:173
  56.5 37.7 %collective-permute-start.24 = (bf16[2,4,224,512]{3,2,1,0:T(8,128)(2,1)S(1)}, bf16[2,4,224,512]{3,2,1,0:T(8,128)(2,1)S(1)}, u32[]{:S(2)}, u32[]{:S(2)}) collective-permute-start(bf16[2,4,224,512]{3,2,1,0:T(8,128)(2,1)S(1)} %pad_maximum_fusion.1.rest_0_), channel_id=1, source_target_pairs={{0,3},{1,0},{2,1},{3,2},{4,7},{5,4},{6,5},{7,6},{8,11},{9,8},{10,9... | collective-permute-start | bytes 5505032 | tf_op jit(solution)/shard_map/ppermute | solution.py:172
  59.4 38.4 %collective-permute-start.22 = (bf16[2,4,224,512]{3,2,1,0:T(8,128)(2,1)S(1)}, bf16[2,4,224,512]{3,2,1,0:T(8,128)(2,1)S(1)}, u32[]{:S(2)}, u32[]{:S(2)}) collective-permute-start(bf16[2,4,224,512]{3,2,1,0:T(8,128)(2,1)S(1)} %pad_maximum_fusion.1.rest_0_), channel_id=1, source_target_pairs={{0,1},{1,2},{2,3},{3,0},{4,5},{5,6},{6,7},{7,4},{8,9},{9,10},{10,1... | collective-permute-start | bytes 5505032 | tf_op jit(solution)/shard_map/ppermute | solution.py:172
  59.9 39.0 %collective-permute-start.12 = (bf16[2,4,224,512]{3,2,1,0:T(8,128)(2,1)S(1)}, bf16[2,4,224,512]{3,2,1,0:T(8,128)(2,1)S(1)}, u32[]{:S(2)}, u32[]{:S(2)}) collective-permute-start(bf16[2,4,224,512]{3,2,1,0:T(8,128)(2,1)S(1)} %pad_maximum_fusion.rest_0_), channel_id=1, source_target_pairs={{0,12},{1,13},{2,14},{3,15},{4,0},{5,1},{6,2},{7,3},{8,4},{9,5},{1... | collective-permute-start | bytes 5505032 | tf_op jit(solution)/shard_map/ppermute | solution.py:172
  60.0 41.8 %collective-permute-start.10 = (bf16[2,4,224,512]{3,2,1,0:T(8,128)(2,1)S(1)}, bf16[2,4,224,512]{3,2,1,0:T(8,128)(2,1)S(1)}, u32[]{:S(2)}, u32[]{:S(2)}) collective-permute-start(bf16[2,4,224,512]{3,2,1,0:T(8,128)(2,1)S(1)} %pad_maximum_fusion.rest_0_), channel_id=1, source_target_pairs={{0,4},{1,5},{2,6},{3,7},{4,8},{5,9},{6,10},{7,11},{8,12},{9,13},{1... | collective-permute-start | bytes 5505032 | tf_op jit(solution)/shard_map/ppermute | solution.py:172
  94.2 4.7 %copy-start.2 = (bf16[2,4,224,512]{3,2,1,0:T(8,128)(2,1)}, bf16[2,4,224,512]{3,2,1,0:T(8,128)(2,1)S(1)}, u32[]{:S(2)}) copy-start(bf16[2,4,224,512]{3,2,1,0:T(8,128)(2,1)S(1)} %collective-permute-done.24.rest_2_) | copy-start | bytes 5505028
  94.3 22.8 %collective-permute-start.25 = (bf16[4,224,512]{2,1,0:T(8,128)(2,1)S(1)}, bf16[4,224,512]{2,1,0:T(8,128)(2,1)S(1)}, u32[]{:S(2)}, u32[]{:S(2)}) collective-permute-start(bf16[4,224,512]{2,1,0:T(8,128)(2,1)S(1)} %slice_bitcast_fusion), channel_id=1, source_target_pairs={{0,3},{1,0},{2,1},{3,2},{4,7},{5,4},{6,5},{7,6},{8,11},{9,8},{10,9... | collective-permute-start | bytes 2752520 | tf_op jit(solution)/shard_map/ppermute | solution.py:173
  97.8 2.4 %copy-start.3 = (bf16[2,4,224,512]{3,2,1,0:T(8,128)(2,1)}, bf16[2,4,224,512]{3,2,1,0:T(8,128)(2,1)S(1)}, u32[]{:S(2)}) copy-start(bf16[2,4,224,512]{3,2,1,0:T(8,128)(2,1)S(1)} %collective-permute-done.22.rest_1_) | copy-start | bytes 5505028
  98.9 18.2 %collective-permute-start.23 = (bf16[4,224,512]{2,1,0:T(8,128)(2,1)}, bf16[4,224,512]{2,1,0:T(8,128)(2,1)S(1)}, u32[]{:S(2)}, u32[]{:S(2)}) collective-permute-start(bf16[4,224,512]{2,1,0:T(8,128)(2,1)} %slice_bitcast_fusion.1), channel_id=1, source_target_pairs={{0,1},{1,2},{2,3},{3,0},{4,5},{5,6},{6,7},{7,4},{8,9},{9,10},{10,1... | collective-permute-start | bytes 2752520 | tf_op jit(solution)/shard_map/ppermute | solution.py:173
  98.9 1.2 copy-start.4
  100.2 30.8 %collective-permute-start.13 = (bf16[4,224,512]{2,1,0:T(8,128)(2,1)S(1)}, bf16[4,224,512]{2,1,0:T(8,128)(2,1)S(1)}, u32[]{:S(2)}, u32[]{:S(2)}) collective-permute-start(bf16[4,224,512]{2,1,0:T(8,128)(2,1)S(1)} %slice_bitcast_fusion.2), channel_id=1, source_target_pairs={{0,12},{1,13},{2,14},{3,15},{4,0},{5,1},{6,2},{7,3},{8,4},{9,5},{1... | collective-permute-start | bytes 2752520 | tf_op jit(solution)/shard_map/ppermute | solution.py:173
  101.8 1.2 copy-start.5
  101.9 29.1 %collective-permute-start.11 = (bf16[4,224,512]{2,1,0:T(8,128)(2,1)S(1)}, bf16[4,224,512]{2,1,0:T(8,128)(2,1)S(1)}, u32[]{:S(2)}, u32[]{:S(2)}) collective-permute-start(bf16[4,224,512]{2,1,0:T(8,128)(2,1)S(1)} %slice_bitcast_fusion.3), channel_id=1, source_target_pairs={{0,4},{1,5},{2,6},{3,7},{4,8},{5,9},{6,10},{7,11},{8,12},{9,13},{1... | collective-permute-start | bytes 2752520 | tf_op jit(solution)/shard_map/ppermute | solution.py:173
  121.0 18.9 %collective-permute-start.27 = (bf16[448,128]{1,0:T(8,128)(2,1)S(1)}, bf16[448,128]{1,0:T(8,128)(2,1)S(1)}, u32[]{:S(2)}, u32[]{:S(2)}) collective-permute-start(bf16[448,128]{1,0:T(8,128)(2,1)S(1)} %get-tuple-element.43), channel_id=1, source_target_pairs={{0,192},{16,208},{32,224},{48,240},{64,0},{80,16},{96,32},{112,48}... | collective-permute-start | bytes 344072 | tf_op jit(solution)/shard_map/ppermute | solution.py:215
  127.8 13.7 %collective-permute-start.28 = (bf16[448,128]{1,0:T(8,128)(2,1)S(1)}, bf16[448,128]{1,0:T(8,128)(2,1)S(1)}, u32[]{:S(2)}, u32[]{:S(2)}) collective-permute-start(bf16[448,128]{1,0:T(8,128)(2,1)S(1)} %get-tuple-element.44), channel_id=1, source_target_pairs={{0,160},{16,176},{32,192},{48,208},{64,224},{80,240},{96,0},{112,1... | collective-permute-start | bytes 344072 | tf_op jit(solution)/shard_map/ppermute | solution.py:215
  129.4 12.7 %collective-permute-start.30 = (bf16[448,128]{1,0:T(8,128)(2,1)S(1)}, bf16[448,128]{1,0:T(8,128)(2,1)S(1)}, u32[]{:S(2)}, u32[]{:S(2)}) collective-permute-start(bf16[448,128]{1,0:T(8,128)(2,1)S(1)} %get-tuple-element.46), channel_id=1, source_target_pairs={{0,96},{16,112},{32,128},{48,144},{64,160},{80,176},{96,192},{112,... | collective-permute-start | bytes 344072 | tf_op jit(solution)/shard_map/ppermute | solution.py:215
  131.0 11.1 %collective-permute-start.31 = (bf16[448,128]{1,0:T(8,128)(2,1)S(1)}, bf16[448,128]{1,0:T(8,128)(2,1)S(1)}, u32[]{:S(2)}, u32[]{:S(2)}) collective-permute-start(bf16[448,128]{1,0:T(8,128)(2,1)S(1)} %get-tuple-element.47), channel_id=1, source_target_pairs={{0,64},{16,80},{32,96},{48,112},{64,128},{80,144},{96,160},{112,17... | collective-permute-start | bytes 344072 | tf_op jit(solution)/shard_map/ppermute | solution.py:215
  134.9 8.7 %collective-permute-start.26 = (bf16[448,128]{1,0:T(8,128)(2,1)S(1)}, bf16[448,128]{1,0:T(8,128)(2,1)S(1)}, u32[]{:S(2)}, u32[]{:S(2)}) collective-permute-start(bf16[448,128]{1,0:T(8,128)(2,1)S(1)} %get-tuple-element.40), channel_id=1, source_target_pairs={{0,224},{16,240},{32,0},{48,16},{64,32},{80,48},{96,64},{112,80},{... | collective-permute-start | bytes 344072 | tf_op jit(solution)/shard_map/ppermute | solution.py:215
  139.9 9.7 %collective-permute-start.29 = (bf16[448,128]{1,0:T(8,128)(2,1)S(1)}, bf16[448,128]{1,0:T(8,128)(2,1)S(1)}, u32[]{:S(2)}, u32[]{:S(2)}) collective-permute-start(bf16[448,128]{1,0:T(8,128)(2,1)S(1)} %get-tuple-element.45), channel_id=1, source_target_pairs={{0,128},{16,144},{32,160},{48,176},{64,192},{80,208},{96,224},{112... | collective-permute-start | bytes 344072 | tf_op jit(solution)/shard_map/ppermute | solution.py:215
  141.4 8.9 %collective-permute-start.32 = (bf16[448,128]{1,0:T(8,128)(2,1)S(1)}, bf16[448,128]{1,0:T(8,128)(2,1)S(1)}, u32[]{:S(2)}, u32[]{:S(2)}) collective-permute-start(bf16[448,128]{1,0:T(8,128)(2,1)S(1)} %get-tuple-element.48), channel_id=1, source_target_pairs={{0,32},{16,48},{32,64},{48,80},{64,96},{80,112},{96,128},{112,144}... | collective-permute-start | bytes 344072 | tf_op jit(solution)/shard_map/ppermute | solution.py:215
  151.6 6.7 %collective-permute-start.33 = (f32[128,448]{1,0:T(8,128)S(1)}, f32[128,448]{1,0:T(8,128)S(1)}, u32[]{:S(2)}, u32[]{:S(2)}) collective-permute-start(f32[128,448]{1,0:T(8,128)S(1)} %get-tuple-element.50), channel_id=1, source_target_pairs={{0,16},{16,0},{32,48},{48,32},{64,80},{80,64},{96,112},{112,96},{1... | collective-permute-start | bytes 688136 | tf_op jit(solution)/shard_map/ppermute | solution.py:211

commit v3 on v2

--- a/solution.py
+++ b/solution.py
@@ -100,15 +100,14 @@
     x, y = panel // SIDE, panel % SIDE
     feat, half = held.shape[1], held.shape[1] // 2
     width = gathered.shape[2]
-    copies = []
+    copies, blanks = [], []
     for g, second in enumerate(range(SIDE - 1) if early else (SIDE - 1,)):
         for first in range(SIDE):
             dx, dy = (STEPS[first], STEPS[second]) if x_first else (STEPS[second], STEPS[first])
             owner = (x + dx + SIDE) % SIDE * SIDE + (y + dy + SIDE) % SIDE
             lead = owner % 2 * (WINDOW - feat)
             top = first * WINDOW
-            gathered[g, pl.ds(top, WINDOW - feat), :] = jnp.zeros((WINDOW - feat, width), gathered.dtype)
-            gathered[g, pl.ds(top + feat, WINDOW - feat), :] = jnp.zeros((WINDOW - feat, width), gathered.dtype)
+            blanks.append((g, pl.multiple_of(top + (1 - owner % 2) * feat, 16)))
             columns = pl.ds(pl.multiple_of(owner * feat - lead, 128), WINDOW)
             window = held.at[g, :, pl.ds(top, WINDOW)]
             copies.append(pltpu.make_async_copy(factor.at[:, columns], window, sems.at[len(copies)]))
@@ -118,6 +117,8 @@
                 target = gathered.at[g, pl.ds(pl.multiple_of(top + j * half + lead, 16), half)]
                 copies.append(pltpu.make_async_copy(source, target, sems.at[len(copies)]))
                 copies[-1].start()
+    for g, top in blanks:
+        gathered[g, pl.ds(top, WINDOW - feat), :] = jnp.zeros((WINDOW - feat, width), gathered.dtype)
     count = len(copies) // held.shape[0]
     if early:
         for g in range(held.shape[0]):
@@ -127,10 +128,10 @@
             outs[0][...] = total if g == 0 else total + outs[0][...]
         return
     total = before[0][...]
-    for first in range(SIDE):
-        for copy in copies[first * 3 : first * 3 + 3]:
+    for first in range(0, SIDE, 2):
+        for copy in copies[first * 3 : first * 3 + 6]:
             copy.wait()
-        span = pl.ds(first * WINDOW, WINDOW)
+        span = pl.ds(first * WINDOW, 2 * WINDOW)
         total += dot(held[0, :, span], gathered[0, span, :])
     total = total.astype(jnp.bfloat16)
     for b, block in enumerate(outs):

time: 159 us -> 159 us (level)
  no operation moved by 1% of the time
where the time goes in v3:
time: 159 us
  starting transfers between devices  65.4 us (41%)
  waiting for transfers between devices  59.4 us (37%)
  Pallas kernels  25.5 us (16%)
  local copies, waits for them, and re-layouts  7.24 us (5%)
    ppermute x8, waiting for transfers between devices, go_round(): behind, ahead = (lax.ppermute(parts, 'panel', way(by)) for by in (1, -1))  37.5 us
    ppermute x14, starting transfers between devices, on_device(): lax.ppermute(a, 'expert', along_z(k))  33.3 us
    pallas_call x4, Pallas kernels, times_ring(): pl.pallas_call(functools.partial(ring_kernel, x_first, early), in_specs=[...  21.5 us
    ppermute x14, waiting for transfers between devices, on_device(): lax.ppermute(a, 'expert', along_z(k))  14.9 us
    ppermute x4, starting transfers between devices, go_round(): lax.ppermute(ahead[1], 'panel', way(-1))  11.4 us
    ppermute x8, starting transfers between devices, go_round(): behind, ahead = (lax.ppermute(parts, 'panel', way(by)) for by in (1, -1))  9.84 us
    ppermute x4, starting transfers between devices, on_device(): swap = lambda a: lax.ppermute(a, 'expert', SWAP)  9.16 us
    unnamed x19, local copies, waits for them, and re-layouts  4.83 us
  transfers between devices with their start and end apart: 34, of which 11 were waited for; matrix products, arithmetic and copies ran while one was open for 2% of the time, Pallas kernels for 14%

profile of v3, /device:TPU:1, one launch (start us, length us, event | category | flops | bytes accessed | tf_op | source)
XLA Modules:
  0.0 158.8 jit_solution(12105375919650156743)
XLA Ops:
  0.0 1.2 copy.5
  1.2 3.3 %collective-permute-start.2 = (bf16[4,128,448]{2,1,0:T(8,128)(2,1)S(1)}, bf16[4,128,448]{2,1,0:T(8,128)(2,1)S(1)}, u32[]{:S(2)}, u32[]{:S(2)}) collective-permute-start(bf16[4,128,448]{2,1,0:T(8,128)(2,1)S(1)} %bitcast.42), channel_id=1, source_target_pairs={{0,16},{16,0},{32,48},{48,32},{64,80},{80,64},{96,112},{112,96},{1... | collective-permute-start | bytes 1376264 | tf_op jit(solution)/shard_map/ppermute | solution.py:212
  4.6 0.1 collective-permute-start
  4.7 0.4 collective-permute-start.1
  5.1 1.2 collective-permute-done.other_ids
  6.3 0.7 copy-done
  7.0 0.7 copy-done.1
  7.7 2.8 %route.1 = (bf16[448,128]{1,0:T(8,128)(2,1)S(1)}, bf16[448,128]{1,0:T(8,128)(2,1)S(1)}, bf16[448,128]{1,0:T(8,128)(2,1)S(1)}, bf16[448,128]{1,0:T(8,128)(2,1)S(1...) custom-call(s32[4,128]{1,0:T(4,128)S(1)} %bitcast.45, ...), custom_call_target="tpu_custom_call" | custom-call | tf_op jit(solution)/shard_map/route/pallas_call | solution.py:83
  10.5 0.1 collective-permute-start.3
  10.6 3.9 %collective-permute-start.4 = (bf16[448,128]{1,0:T(8,128)(2,1)S(1)}, bf16[448,128]{1,0:T(8,128)(2,1)S(1)}, u32[]{:S(2)}, u32[]{:S(2)}) collective-permute-start(bf16[448,128]{1,0:T(8,128)(2,1)S(1)} %get-tuple-element.32), channel_id=1, source_target_pairs={{0,224},{16,240},{32,0},{48,16},{64,32},{80,48},{96,64},{112,80},{... | collective-permute-start | bytes 344072 | tf_op jit(solution)/shard_map/ppermute | solution.py:216
  14.5 3.9 %collective-permute-start.5 = (bf16[448,128]{1,0:T(8,128)(2,1)S(1)}, bf16[448,128]{1,0:T(8,128)(2,1)S(1)}, u32[]{:S(2)}, u32[]{:S(2)}) collective-permute-start(bf16[448,128]{1,0:T(8,128)(2,1)S(1)} %get-tuple-element.33), channel_id=1, source_target_pairs={{0,128},{16,144},{32,160},{48,176},{64,192},{80,208},{96,224},{112... | collective-permute-start | bytes 344072 | tf_op jit(solution)/shard_map/ppermute | solution.py:216
  18.4 3.6 %collective-permute-start.15 = (bf16[448,128]{1,0:T(8,128)(2,1)S(1)}, bf16[448,128]{1,0:T(8,128)(2,1)S(1)}, u32[]{:S(2)}, u32[]{:S(2)}) collective-permute-start(bf16[448,128]{1,0:T(8,128)(2,1)S(1)} %get-tuple-element.35), channel_id=1, source_target_pairs={{0,192},{16,208},{32,224},{48,240},{64,0},{80,16},{96,32},{112,48}... | collective-permute-start | bytes 344072 | tf_op jit(solution)/shard_map/ppermute | solution.py:216
  22.0 0.1 collective-permute-start.16
  22.1 4.5 %collective-permute-start.17 = (bf16[448,128]{1,0:T(8,128)(2,1)S(1)}, bf16[448,128]{1,0:T(8,128)(2,1)S(1)}, u32[]{:S(2)}, u32[]{:S(2)}) collective-permute-start(bf16[448,128]{1,0:T(8,128)(2,1)S(1)} %get-tuple-element.37), channel_id=1, source_target_pairs={{0,160},{16,176},{32,192},{48,208},{64,224},{80,240},{96,0},{112,1... | collective-permute-start | bytes 344072 | tf_op jit(solution)/shard_map/ppermute | solution.py:216
  26.8 2.8 %collective-permute-start.7 = (bf16[2,224,512]{2,1,0:T(8,128)(2,1)S(1)}, bf16[2,224,512]{2,1,0:T(8,128)(2,1)S(1)}, u32[]{:S(2)}, u32[]{:S(2)}) collective-permute-start(bf16[2,224,512]{2,1,0:T(8,128)(2,1)S(1)} %bitcast.52), channel_id=1, source_target_pairs={{0,3},{1,0},{2,1},{3,2},{4,7},{5,4},{6,5},{7,6},{8,11},{9,8},{10,9... | collective-permute-start | bytes 1376264 | tf_op jit(solution)/shard_map/ppermute | solution.py:173
  29.6 1.5 collective-permute-done.15
  31.1 5.0 %collective-permute-done.16 = bf16[448,128]{1,0:T(8,128)(2,1)S(1)} collective-permute-done((bf16[448,128]{1,0:T(8,128)(2,1)S(1)}, bf16[448,128]{1,0:T(8,128)(2,1)S(1)}, u32[]{:S(2)}, u32[]{:S(2)}) %collective-permute-start.16) | collective-permute-done | bytes 114720 | tf_op jit(solution)/shard_map/ppermute | solution.py:216
  36.2 2.6 %collective-permute-start.19 = (bf16[2,224,512]{2,1,0:T(8,128)(2,1)S(1)}, bf16[2,224,512]{2,1,0:T(8,128)(2,1)S(1)}, u32[]{:S(2)}, u32[]{:S(2)}) collective-permute-start(bf16[2,224,512]{2,1,0:T(8,128)(2,1)S(1)} %bitcast.54), channel_id=1, source_target_pairs={{0,12},{1,13},{2,14},{3,15},{4,0},{5,1},{6,2},{7,3},{8,4},{9,5},{1... | collective-permute-start | bytes 1376264 | tf_op jit(solution)/shard_map/ppermute | solution.py:173
  38.8 0.1 fusion.3
  38.8 2.8 %collective-permute-start.9 = (bf16[224,512]{1,0:T(8,128)(2,1)S(1)}, bf16[224,512]{1,0:T(8,128)(2,1)S(1)}, u32[]{:S(2)}, u32[]{:S(2)}) collective-permute-start(bf16[224,512]{1,0:T(8,128)(2,1)S(1)} %get-tuple-element.65), channel_id=1, source_target_pairs={{0,3},{1,0},{2,1},{3,2},{4,7},{5,4},{6,5},{7,6},{8,11},{9,8},{10,9... | collective-permute-start | bytes 688136 | tf_op jit(solution)/shard_map/ppermute | solution.py:174
  41.7 4.8 %collective-permute-done.19 = bf16[2,224,512]{2,1,0:T(8,128)(2,1)S(1)} collective-permute-done((bf16[2,224,512]{2,1,0:T(8,128)(2,1)S(1)}, bf16[2,224,512]{2,1,0:T(8,128)(2,1)S(1)}, u32[]{:S(2)}, u32[]{:S(2)}) %collective-permute-start.19) | collective-permute-done | bytes 458784 | tf_op jit(solution)/shard_map/ppermute | solution.py:173
  46.5 3.5 %collective-permute-start.21 = (bf16[224,512]{1,0:T(8,128)(2,1)S(1)}, bf16[224,512]{1,0:T(8,128)(2,1)S(1)}, u32[]{:S(2)}, u32[]{:S(2)}) collective-permute-start(bf16[224,512]{1,0:T(8,128)(2,1)S(1)} %get-tuple-element.57), channel_id=1, source_target_pairs={{0,12},{1,13},{2,14},{3,15},{4,0},{5,1},{6,2},{7,3},{8,4},{9,5},{1... | collective-permute-start | bytes 688136 | tf_op jit(solution)/shard_map/ppermute | solution.py:174
  50.0 0.1 collective-permute-start.20
  50.1 0.1 fusion.2
  50.2 1.3 collective-permute-start.8
  51.5 1.4 collective-permute-done.21
  52.9 0.1 maximum_bitcast_fusion.3
  53.0 3.1 %collective-permute-done.20 = bf16[224,512]{1,0:T(8,128)(2,1)S(1)} collective-permute-done((bf16[224,512]{1,0:T(8,128)(2,1)S(1)}, bf16[224,512]{1,0:T(8,128)(2,1)S(1)}, u32[]{:S(2)}, u32[]{:S(2)}) %collective-permute-start.20) | collective-permute-done | bytes 229408 | tf_op jit(solution)/shard_map/ppermute | solution.py:174
  56.2 0.1 maximum_bitcast_fusion.2
  56.3 0.2 pad_maximum_fusion.1.rest_0_
  56.5 2.9 %collective-permute-start.24 = (bf16[2,4,224,512]{3,2,1,0:T(8,128)(2,1)S(1)}, bf16[2,4,224,512]{3,2,1,0:T(8,128)(2,1)S(1)}, u32[]{:S(2)}, u32[]{:S(2)}) collective-permute-start(bf16[2,4,224,512]{3,2,1,0:T(8,128)(2,1)S(1)} %pad_maximum_fusion.1.rest_0_), channel_id=1, source_target_pairs={{0,3},{1,0},{2,1},{3,2},{4,7},{5,4},{6,5},{7,6},{8,11},{9,8},{10,9... | collective-permute-start | bytes 5505032 | tf_op jit(solution)/shard_map/ppermute | solution.py:173
  59.4 0.1 collective-permute-start.22
  59.5 0.1 maximum_bitcast_fusion.1
  59.6 0.1 maximum_bitcast_fusion
  59.7 0.2 pad_maximum_fusion.rest_0_
  59.9 0.1 collective-permute-start.12
  60.0 1.5 collective-permute-start.10
  61.5 32.7 %collective-permute-done.24.rest_2_ = bf16[2,4,224,512]{3,2,1,0:T(8,128)(2,1)S(1)} collective-permute-done((bf16[2,4,224,512]{3,2,1,0:T(8,128)(2,1)S(1)}, bf16[2,4,224,512]{3,2,1,0:T(8,128)(2,1)S(1)}, u32[]{:S(2)}, u32[]{:S(2)}) %collective-permute-start.24) | collective-permute-done | bytes 1835040 | tf_op jit(solution)/shard_map/ppermute | solution.py:173
  94.2 0.1 slice_bitcast_fusion
  94.3 3.5 %collective-permute-start.25 = (bf16[4,224,512]{2,1,0:T(8,128)(2,1)S(1)}, bf16[4,224,512]{2,1,0:T(8,128)(2,1)S(1)}, u32[]{:S(2)}, u32[]{:S(2)}) collective-permute-start(bf16[4,224,512]{2,1,0:T(8,128)(2,1)S(1)} %slice_bitcast_fusion), channel_id=1, source_target_pairs={{0,3},{1,0},{2,1},{3,2},{4,7},{5,4},{6,5},{7,6},{8,11},{9,8},{10,9... | collective-permute-start | bytes 2752520 | tf_op jit(solution)/shard_map/ppermute | solution.py:174
  97.8 1.1 slice_bitcast_fusion.1
  98.9 1.2 copy-done.4
  100.1 0.1 slice_bitcast_fusion.2
  100.2 1.6 %collective-permute-start.13 = (bf16[4,224,512]{2,1,0:T(8,128)(2,1)S(1)}, bf16[4,224,512]{2,1,0:T(8,128)(2,1)S(1)}, u32[]{:S(2)}, u32[]{:S(2)}) collective-permute-start(bf16[4,224,512]{2,1,0:T(8,128)(2,1)S(1)} %slice_bitcast_fusion.2), channel_id=1, source_target_pairs={{0,12},{1,13},{2,14},{3,15},{4,0},{5,1},{6,2},{7,3},{8,4},{9,5},{1... | collective-permute-start | bytes 2752520 | tf_op jit(solution)/shard_map/ppermute | solution.py:174
  101.8 0.1 slice_bitcast_fusion.3
  101.9 0.3 collective-permute-start.11
  102.2 0.9 copy-done.5
  103.1 6.9 %times_ring_early.3.rest_2_ = f32[448,512]{1,0:T(8,128)S(1)} custom-call(bf16[448,7168]{1,0:T(8,128)(2,1)} %bitcast.48, bf16[2,4,224,512]{3,2,1,0:T(8,128)(2,1)S(1)} %pad_maximum_fusion.1.rest_0_, bf16[2,4,224,512]{3,2,1,0:T(8,128)(2,1)} %copy-done.3, bf16[2,4,224,512]{3,2,1,0:T(8,128)(2,1)} %copy-done.2), custom_call_target="tpu_custom_call" | custom-call | flops 2818572288 | bytes 11796480 | tf_op jit(solution)/shard_map/times_ring_early/pallas_call | solution.py:152
  110.0 7.0 %times_ring_early.2.rest_2_ = f32[448,512]{1,0:T(8,128)S(1)} custom-call(bf16[448,7168]{1,0:T(8,128)(2,1)} %bitcast.49, bf16[2,4,224,512]{3,2,1,0:T(8,128)(2,1)S(1)} %pad_maximum_fusion.rest_0_, bf16[2,4,224,512]{3,2,1,0:T(8,128)(2,1)} %copy-done.5, bf16[2,4,224,512]{3,2,1,0:T(8,128)(2,1)} %copy-done.4), custom_call_target="tpu_custom_call" | custom-call | flops 2818572288 | bytes 11796480 | tf_op jit(solution)/shard_map/times_ring_early/pallas_call | solution.py:152
  117.0 3.8 %times_ring_late.3 = (bf16[448,128]{1,0:T(8,128)(2,1)S(1)}, bf16[448,128]{1,0:T(8,128)(2,1)S(1)}, bf16[448,128]{1,0:T(8,128)(2,1)S(1)}, bf16[448,128]{1,0:T(8,128)(2,1)S(1)}) custom-call(bf16[448,7168]{1,0:T(8,128)(2,1)} %bitcast.50, bf16[4,224,512]{2,1,0:T(8,128)(2,1)S(1)} %collective-permute-done.23.rest_0_, ...), custom_call_target="tpu_custom_call" | custom-call | flops 939524096 | bytes 3932160 | tf_op jit(solution)/shard_map/times_ring_late/pallas_call | solution.py:152
  120.8 6.8 %collective-permute-start.27 = (bf16[448,128]{1,0:T(8,128)(2,1)S(1)}, bf16[448,128]{1,0:T(8,128)(2,1)S(1)}, u32[]{:S(2)}, u32[]{:S(2)}) collective-permute-start(bf16[448,128]{1,0:T(8,128)(2,1)S(1)} %get-tuple-element.43), channel_id=1, source_target_pairs={{0,192},{16,208},{32,224},{48,240},{64,0},{80,16},{96,32},{112,48}... | collective-permute-start | bytes 344072 | tf_op jit(solution)/shard_map/ppermute | solution.py:216
  127.6 1.6 %collective-permute-start.28 = (bf16[448,128]{1,0:T(8,128)(2,1)S(1)}, bf16[448,128]{1,0:T(8,128)(2,1)S(1)}, u32[]{:S(2)}, u32[]{:S(2)}) collective-permute-start(bf16[448,128]{1,0:T(8,128)(2,1)S(1)} %get-tuple-element.44), channel_id=1, source_target_pairs={{0,160},{16,176},{32,192},{48,208},{64,224},{80,240},{96,0},{112,1... | collective-permute-start | bytes 344072 | tf_op jit(solution)/shard_map/ppermute | solution.py:216
  129.2 1.6 %collective-permute-start.30 = (bf16[448,128]{1,0:T(8,128)(2,1)S(1)}, bf16[448,128]{1,0:T(8,128)(2,1)S(1)}, u32[]{:S(2)}, u32[]{:S(2)}) collective-permute-start(bf16[448,128]{1,0:T(8,128)(2,1)S(1)} %get-tuple-element.46), channel_id=1, source_target_pairs={{0,96},{16,112},{32,128},{48,144},{64,160},{80,176},{96,192},{112,... | collective-permute-start | bytes 344072 | tf_op jit(solution)/shard_map/ppermute | solution.py:216
  130.9 3.8 %times_ring_late.2 = (bf16[448,128]{1,0:T(8,128)(2,1)S(1)}, bf16[448,128]{1,0:T(8,128)(2,1)S(1)}, bf16[448,128]{1,0:T(8,128)(2,1)S(1)}, bf16[448,128]{1,0:T(8,128)(2,1)S(1)}) custom-call(bf16[448,7168]{1,0:T(8,128)(2,1)} %bitcast.51, bf16[4,224,512]{2,1,0:T(8,128)(2,1)S(1)} %collective-permute-done.11.rest_0_, ...), custom_call_target="tpu_custom_call" | custom-call | flops 939524096 | bytes 3932160 | tf_op jit(solution)/shard_map/times_ring_late/pallas_call | solution.py:152
  134.7 5.0 %collective-permute-start.26 = (bf16[448,128]{1,0:T(8,128)(2,1)S(1)}, bf16[448,128]{1,0:T(8,128)(2,1)S(1)}, u32[]{:S(2)}, u32[]{:S(2)}) collective-permute-start(bf16[448,128]{1,0:T(8,128)(2,1)S(1)} %get-tuple-element.40), channel_id=1, source_target_pairs={{0,224},{16,240},{32,0},{48,16},{64,32},{80,48},{96,64},{112,80},{... | collective-permute-start | bytes 344072 | tf_op jit(solution)/shard_map/ppermute | solution.py:216
  139.6 1.5 collective-permute-start.29
  141.1 0.7 collective-permute-start.32
  141.8 1.7 %collective-permute-done.26.rest_1_ = bf16[448,128]{1,0:T(8,128)(2,1)S(1)} collective-permute-done((bf16[448,128]{1,0:T(8,128)(2,1)S(1)}, bf16[448,128]{1,0:T(8,128)(2,1)S(1)}, u32[]{:S(2)}, u32[]{:S(2)}) %collective-permute-start.26) | collective-permute-done | bytes 114720 | tf_op jit(solution)/shard_map/ppermute | solution.py:216
  143.5 5.7 %collective-permute-done.29.rest_4_ = bf16[448,128]{1,0:T(8,128)(2,1)S(1)} collective-permute-done((bf16[448,128]{1,0:T(8,128)(2,1)S(1)}, bf16[448,128]{1,0:T(8,128)(2,1)S(1)}, u32[]{:S(2)}, u32[]{:S(2)}) %collective-permute-start.29) | collective-permute-done | bytes 114720 | tf_op jit(solution)/shard_map/ppermute | solution.py:216
  149.2 1.0 collective-permute-done.32.rest_7_
  150.2 1.2 combine.1
  151.5 5.3 %collective-permute-start.33 = (f32[128,448]{1,0:T(8,128)S(1)}, f32[128,448]{1,0:T(8,128)S(1)}, u32[]{:S(2)}, u32[]{:S(2)}) collective-permute-start(f32[128,448]{1,0:T(8,128)S(1)} %get-tuple-element.50), channel_id=1, source_target_pairs={{0,16},{16,0},{32,48},{48,32},{64,80},{80,64},{96,112},{112,96},{1... | collective-permute-start | bytes 688136 | tf_op jit(solution)/shard_map/ppermute | solution.py:212
  156.8 1.2 collective-permute-done.33
  158.0 0.8 copy.6
  (49 shorter events, 0.5 us)
Async XLA Ops:
  1.2 5.1 %collective-permute-start.2 = (bf16[4,128,448]{2,1,0:T(8,128)(2,1)S(1)}, bf16[4,128,448]{2,1,0:T(8,128)(2,1)S(1)}, u32[]{:S(2)}, u32[]{:S(2)}) collective-permute-start(bf16[4,128,448]{2,1,0:T(8,128)(2,1)S(1)} %bitcast.42), channel_id=1, source_target_pairs={{0,16},{16,0},{32,48},{48,32},{64,80},{80,64},{96,112},{112,96},{1... | collective-permute-start | bytes 1376264 | tf_op jit(solution)/shard_map/ppermute | solution.py:212
  4.6 1.8 %collective-permute-start = (s32[4,128]{1,0:T(4,128)}, s32[4,128]{1,0:T(4,128)S(1)}, u32[]{:S(2)}, u32[]{:S(2)}) collective-permute-start(s32[4,128]{1,0:T(4,128)} %bitcast.44), channel_id=1, source_target_pairs={{0,16},{16,0},{32,48},{48,32},{64,80},{80,64},{96,112},{112,96},{1... | collective-permute-start | bytes 6152 | tf_op jit(solution)/shard_map/ppermute | solution.py:212
  4.7 1.7 %collective-permute-start.1 = (f32[4,128]{1,0:T(4,128)}, f32[4,128]{1,0:T(4,128)S(1)}, u32[]{:S(2)}, u32[]{:S(2)}) collective-permute-start(f32[4,128]{1,0:T(4,128)} %bitcast.46), channel_id=1, source_target_pairs={{0,16},{16,0},{32,48},{48,32},{64,80},{80,64},{96,112},{112,96},{1... | collective-permute-start | bytes 6152 | tf_op jit(solution)/shard_map/ppermute | solution.py:212
  6.3 0.7 copy-start
  7.0 0.7 copy-start.1
  10.5 11.5 %collective-permute-start.3 = (bf16[448,128]{1,0:T(8,128)(2,1)S(1)}, bf16[448,128]{1,0:T(8,128)(2,1)S(1)}, u32[]{:S(2)}, u32[]{:S(2)}) collective-permute-start(bf16[448,128]{1,0:T(8,128)(2,1)S(1)} %get-tuple-element.31), channel_id=1, source_target_pairs={{0,32},{16,48},{32,64},{48,80},{64,96},{80,112},{96,128},{112,144}... | collective-permute-start | bytes 344072 | tf_op jit(solution)/shard_map/ppermute | solution.py:216
  10.6 11.6 %collective-permute-start.4 = (bf16[448,128]{1,0:T(8,128)(2,1)S(1)}, bf16[448,128]{1,0:T(8,128)(2,1)S(1)}, u32[]{:S(2)}, u32[]{:S(2)}) collective-permute-start(bf16[448,128]{1,0:T(8,128)(2,1)S(1)} %get-tuple-element.32), channel_id=1, source_target_pairs={{0,224},{16,240},{32,0},{48,16},{64,32},{80,48},{96,64},{112,80},{... | collective-permute-start | bytes 344072 | tf_op jit(solution)/shard_map/ppermute | solution.py:216
  14.5 12.2 %collective-permute-start.5 = (bf16[448,128]{1,0:T(8,128)(2,1)S(1)}, bf16[448,128]{1,0:T(8,128)(2,1)S(1)}, u32[]{:S(2)}, u32[]{:S(2)}) collective-permute-start(bf16[448,128]{1,0:T(8,128)(2,1)S(1)} %get-tuple-element.33), channel_id=1, source_target_pairs={{0,128},{16,144},{32,160},{48,176},{64,192},{80,208},{96,224},{112... | collective-permute-start | bytes 344072 | tf_op jit(solution)/shard_map/ppermute | solution.py:216
  18.4 11.2 %collective-permute-start.14 = (bf16[448,128]{1,0:T(8,128)(2,1)S(1)}, bf16[448,128]{1,0:T(8,128)(2,1)S(1)}, u32[]{:S(2)}, u32[]{:S(2)}) collective-permute-start(bf16[448,128]{1,0:T(8,128)(2,1)S(1)} %get-tuple-element.34), channel_id=1, source_target_pairs={{0,64},{16,80},{32,96},{48,112},{64,128},{80,144},{96,160},{112,17... | collective-permute-start | bytes 344072 | tf_op jit(solution)/shard_map/ppermute | solution.py:216
  18.4 12.7 %collective-permute-start.15 = (bf16[448,128]{1,0:T(8,128)(2,1)S(1)}, bf16[448,128]{1,0:T(8,128)(2,1)S(1)}, u32[]{:S(2)}, u32[]{:S(2)}) collective-permute-start(bf16[448,128]{1,0:T(8,128)(2,1)S(1)} %get-tuple-element.35), channel_id=1, source_target_pairs={{0,192},{16,208},{32,224},{48,240},{64,0},{80,16},{96,32},{112,48}... | collective-permute-start | bytes 344072 | tf_op jit(solution)/shard_map/ppermute | solution.py:216
  22.0 14.1 %collective-permute-start.16 = (bf16[448,128]{1,0:T(8,128)(2,1)S(1)}, bf16[448,128]{1,0:T(8,128)(2,1)S(1)}, u32[]{:S(2)}, u32[]{:S(2)}) collective-permute-start(bf16[448,128]{1,0:T(8,128)(2,1)S(1)} %get-tuple-element.36), channel_id=1, source_target_pairs={{0,96},{16,112},{32,128},{48,144},{64,160},{80,176},{96,192},{112,... | collective-permute-start | bytes 344072 | tf_op jit(solution)/shard_map/ppermute | solution.py:216
  22.1 14.0 %collective-permute-start.17 = (bf16[448,128]{1,0:T(8,128)(2,1)S(1)}, bf16[448,128]{1,0:T(8,128)(2,1)S(1)}, u32[]{:S(2)}, u32[]{:S(2)}) collective-permute-start(bf16[448,128]{1,0:T(8,128)(2,1)S(1)} %get-tuple-element.37), channel_id=1, source_target_pairs={{0,160},{16,176},{32,192},{48,208},{64,224},{80,240},{96,0},{112,1... | collective-permute-start | bytes 344072 | tf_op jit(solution)/shard_map/ppermute | solution.py:216
  26.8 12.0 %collective-permute-start.7 = (bf16[2,224,512]{2,1,0:T(8,128)(2,1)S(1)}, bf16[2,224,512]{2,1,0:T(8,128)(2,1)S(1)}, u32[]{:S(2)}, u32[]{:S(2)}) collective-permute-start(bf16[2,224,512]{2,1,0:T(8,128)(2,1)S(1)} %bitcast.52), channel_id=1, source_target_pairs={{0,3},{1,0},{2,1},{3,2},{4,7},{5,4},{6,5},{7,6},{8,11},{9,8},{10,9... | collective-permute-start | bytes 1376264 | tf_op jit(solution)/shard_map/ppermute | solution.py:173
  29.6 20.6 %collective-permute-start.6 = (bf16[2,224,512]{2,1,0:T(8,128)(2,1)S(1)}, bf16[2,224,512]{2,1,0:T(8,128)(2,1)S(1)}, u32[]{:S(2)}, u32[]{:S(2)}) collective-permute-start(bf16[2,224,512]{2,1,0:T(8,128)(2,1)S(1)} %bitcast.53), channel_id=1, source_target_pairs={{0,1},{1,2},{2,3},{3,0},{4,5},{5,6},{6,7},{7,4},{8,9},{9,10},{10,1... | collective-permute-start | bytes 1376264 | tf_op jit(solution)/shard_map/ppermute | solution.py:173
  36.2 10.3 %collective-permute-start.19 = (bf16[2,224,512]{2,1,0:T(8,128)(2,1)S(1)}, bf16[2,224,512]{2,1,0:T(8,128)(2,1)S(1)}, u32[]{:S(2)}, u32[]{:S(2)}) collective-permute-start(bf16[2,224,512]{2,1,0:T(8,128)(2,1)S(1)} %bitcast.54), channel_id=1, source_target_pairs={{0,12},{1,13},{2,14},{3,15},{4,0},{5,1},{6,2},{7,3},{8,4},{9,5},{1... | collective-permute-start | bytes 1376264 | tf_op jit(solution)/shard_map/ppermute | solution.py:173
  38.7 11.2 %collective-permute-start.18 = (bf16[2,224,512]{2,1,0:T(8,128)(2,1)S(1)}, bf16[2,224,512]{2,1,0:T(8,128)(2,1)S(1)}, u32[]{:S(2)}, u32[]{:S(2)}) collective-permute-start(bf16[2,224,512]{2,1,0:T(8,128)(2,1)S(1)} %bitcast.55), channel_id=1, source_target_pairs={{0,4},{1,5},{2,6},{3,7},{4,8},{5,9},{6,10},{7,11},{8,12},{9,13},{1... | collective-permute-start | bytes 1376264 | tf_op jit(solution)/shard_map/ppermute | solution.py:173
  38.8 20.6 %collective-permute-start.9 = (bf16[224,512]{1,0:T(8,128)(2,1)S(1)}, bf16[224,512]{1,0:T(8,128)(2,1)S(1)}, u32[]{:S(2)}, u32[]{:S(2)}) collective-permute-start(bf16[224,512]{1,0:T(8,128)(2,1)S(1)} %get-tuple-element.65), channel_id=1, source_target_pairs={{0,3},{1,0},{2,1},{3,2},{4,7},{5,4},{6,5},{7,6},{8,11},{9,8},{10,9... | collective-permute-start | bytes 688136 | tf_op jit(solution)/shard_map/ppermute | solution.py:174
  46.5 6.5 %collective-permute-start.21 = (bf16[224,512]{1,0:T(8,128)(2,1)S(1)}, bf16[224,512]{1,0:T(8,128)(2,1)S(1)}, u32[]{:S(2)}, u32[]{:S(2)}) collective-permute-start(bf16[224,512]{1,0:T(8,128)(2,1)S(1)} %get-tuple-element.57), channel_id=1, source_target_pairs={{0,12},{1,13},{2,14},{3,15},{4,0},{5,1},{6,2},{7,3},{8,4},{9,5},{1... | collective-permute-start | bytes 688136 | tf_op jit(solution)/shard_map/ppermute | solution.py:174
  50.0 6.2 %collective-permute-start.20 = (bf16[224,512]{1,0:T(8,128)(2,1)S(1)}, bf16[224,512]{1,0:T(8,128)(2,1)S(1)}, u32[]{:S(2)}, u32[]{:S(2)}) collective-permute-start(bf16[224,512]{1,0:T(8,128)(2,1)S(1)} %get-tuple-element.54), channel_id=1, source_target_pairs={{0,4},{1,5},{2,6},{3,7},{4,8},{5,9},{6,10},{7,11},{8,12},{9,13},{1... | collective-permute-start | bytes 688136 | tf_op jit(solution)/shard_map/ppermute | solution.py:174
  50.2 9.4 %collective-permute-start.8 = (bf16[224,512]{1,0:T(8,128)(2,1)S(1)}, bf16[224,512]{1,0:T(8,128)(2,1)S(1)}, u32[]{:S(2)}, u32[]{:S(2)}) collective-permute-start(bf16[224,512]{1,0:T(8,128)(2,1)S(1)} %get-tuple-element.62), channel_id=1, source_target_pairs={{0,1},{1,2},{2,3},{3,0},{4,5},{5,6},{6,7},{7,4},{8,9},{9,10},{10,1... | collective-permute-start | bytes 688136 | tf_op jit(solution)/shard_map/ppermute | solution.py:174
  56.5 37.7 %collective-permute-start.24 = (bf16[2,4,224,512]{3,2,1,0:T(8,128)(2,1)S(1)}, bf16[2,4,224,512]{3,2,1,0:T(8,128)(2,1)S(1)}, u32[]{:S(2)}, u32[]{:S(2)}) collective-permute-start(bf16[2,4,224,512]{3,2,1,0:T(8,128)(2,1)S(1)} %pad_maximum_fusion.1.rest_0_), channel_id=1, source_target_pairs={{0,3},{1,0},{2,1},{3,2},{4,7},{5,4},{6,5},{7,6},{8,11},{9,8},{10,9... | collective-permute-start | bytes 5505032 | tf_op jit(solution)/shard_map/ppermute | solution.py:173
  59.4 38.4 %collective-permute-start.22 = (bf16[2,4,224,512]{3,2,1,0:T(8,128)(2,1)S(1)}, bf16[2,4,224,512]{3,2,1,0:T(8,128)(2,1)S(1)}, u32[]{:S(2)}, u32[]{:S(2)}) collective-permute-start(bf16[2,4,224,512]{3,2,1,0:T(8,128)(2,1)S(1)} %pad_maximum_fusion.1.rest_0_), channel_id=1, source_target_pairs={{0,1},{1,2},{2,3},{3,0},{4,5},{5,6},{6,7},{7,4},{8,9},{9,10},{10,1... | collective-permute-start | bytes 5505032 | tf_op jit(solution)/shard_map/ppermute | solution.py:173
  59.9 39.0 %collective-permute-start.12 = (bf16[2,4,224,512]{3,2,1,0:T(8,128)(2,1)S(1)}, bf16[2,4,224,512]{3,2,1,0:T(8,128)(2,1)S(1)}, u32[]{:S(2)}, u32[]{:S(2)}) collective-permute-start(bf16[2,4,224,512]{3,2,1,0:T(8,128)(2,1)S(1)} %pad_maximum_fusion.rest_0_), channel_id=1, source_target_pairs={{0,12},{1,13},{2,14},{3,15},{4,0},{5,1},{6,2},{7,3},{8,4},{9,5},{1... | collective-permute-start | bytes 5505032 | tf_op jit(solution)/shard_map/ppermute | solution.py:173
  60.0 41.8 %collective-permute-start.10 = (bf16[2,4,224,512]{3,2,1,0:T(8,128)(2,1)S(1)}, bf16[2,4,224,512]{3,2,1,0:T(8,128)(2,1)S(1)}, u32[]{:S(2)}, u32[]{:S(2)}) collective-permute-start(bf16[2,4,224,512]{3,2,1,0:T(8,128)(2,1)S(1)} %pad_maximum_fusion.rest_0_), channel_id=1, source_target_pairs={{0,4},{1,5},{2,6},{3,7},{4,8},{5,9},{6,10},{7,11},{8,12},{9,13},{1... | collective-permute-start | bytes 5505032 | tf_op jit(solution)/shard_map/ppermute | solution.py:173
  94.2 4.7 %copy-start.2 = (bf16[2,4,224,512]{3,2,1,0:T(8,128)(2,1)}, bf16[2,4,224,512]{3,2,1,0:T(8,128)(2,1)S(1)}, u32[]{:S(2)}) copy-start(bf16[2,4,224,512]{3,2,1,0:T(8,128)(2,1)S(1)} %collective-permute-done.24.rest_2_) | copy-start | bytes 5505028
  94.3 22.7 %collective-permute-start.25 = (bf16[4,224,512]{2,1,0:T(8,128)(2,1)S(1)}, bf16[4,224,512]{2,1,0:T(8,128)(2,1)S(1)}, u32[]{:S(2)}, u32[]{:S(2)}) collective-permute-start(bf16[4,224,512]{2,1,0:T(8,128)(2,1)S(1)} %slice_bitcast_fusion), channel_id=1, source_target_pairs={{0,3},{1,0},{2,1},{3,2},{4,7},{5,4},{6,5},{7,6},{8,11},{9,8},{10,9... | collective-permute-start | bytes 2752520 | tf_op jit(solution)/shard_map/ppermute | solution.py:174
  97.8 2.4 %copy-start.3 = (bf16[2,4,224,512]{3,2,1,0:T(8,128)(2,1)}, bf16[2,4,224,512]{3,2,1,0:T(8,128)(2,1)S(1)}, u32[]{:S(2)}) copy-start(bf16[2,4,224,512]{3,2,1,0:T(8,128)(2,1)S(1)} %collective-permute-done.22.rest_1_) | copy-start | bytes 5505028
  98.9 18.1 %collective-permute-start.23 = (bf16[4,224,512]{2,1,0:T(8,128)(2,1)}, bf16[4,224,512]{2,1,0:T(8,128)(2,1)S(1)}, u32[]{:S(2)}, u32[]{:S(2)}) collective-permute-start(bf16[4,224,512]{2,1,0:T(8,128)(2,1)} %slice_bitcast_fusion.1), channel_id=1, source_target_pairs={{0,1},{1,2},{2,3},{3,0},{4,5},{5,6},{6,7},{7,4},{8,9},{9,10},{10,1... | collective-permute-start | bytes 2752520 | tf_op jit(solution)/shard_map/ppermute | solution.py:174
  98.9 1.2 copy-start.4
  100.2 30.6 %collective-permute-start.13 = (bf16[4,224,512]{2,1,0:T(8,128)(2,1)S(1)}, bf16[4,224,512]{2,1,0:T(8,128)(2,1)S(1)}, u32[]{:S(2)}, u32[]{:S(2)}) collective-permute-start(bf16[4,224,512]{2,1,0:T(8,128)(2,1)S(1)} %slice_bitcast_fusion.2), channel_id=1, source_target_pairs={{0,12},{1,13},{2,14},{3,15},{4,0},{5,1},{6,2},{7,3},{8,4},{9,5},{1... | collective-permute-start | bytes 2752520 | tf_op jit(solution)/shard_map/ppermute | solution.py:174
  101.8 1.2 copy-start.5
  101.9 29.0 %collective-permute-start.11 = (bf16[4,224,512]{2,1,0:T(8,128)(2,1)S(1)}, bf16[4,224,512]{2,1,0:T(8,128)(2,1)S(1)}, u32[]{:S(2)}, u32[]{:S(2)}) collective-permute-start(bf16[4,224,512]{2,1,0:T(8,128)(2,1)S(1)} %slice_bitcast_fusion.3), channel_id=1, source_target_pairs={{0,4},{1,5},{2,6},{3,7},{4,8},{5,9},{6,10},{7,11},{8,12},{9,13},{1... | collective-permute-start | bytes 2752520 | tf_op jit(solution)/shard_map/ppermute | solution.py:174
  120.8 18.8 %collective-permute-start.27 = (bf16[448,128]{1,0:T(8,128)(2,1)S(1)}, bf16[448,128]{1,0:T(8,128)(2,1)S(1)}, u32[]{:S(2)}, u32[]{:S(2)}) collective-permute-start(bf16[448,128]{1,0:T(8,128)(2,1)S(1)} %get-tuple-element.43), channel_id=1, source_target_pairs={{0,192},{16,208},{32,224},{48,240},{64,0},{80,16},{96,32},{112,48}... | collective-permute-start | bytes 344072 | tf_op jit(solution)/shard_map/ppermute | solution.py:216
  127.6 13.5 %collective-permute-start.28 = (bf16[448,128]{1,0:T(8,128)(2,1)S(1)}, bf16[448,128]{1,0:T(8,128)(2,1)S(1)}, u32[]{:S(2)}, u32[]{:S(2)}) collective-permute-start(bf16[448,128]{1,0:T(8,128)(2,1)S(1)} %get-tuple-element.44), channel_id=1, source_target_pairs={{0,160},{16,176},{32,192},{48,208},{64,224},{80,240},{96,0},{112,1... | collective-permute-start | bytes 344072 | tf_op jit(solution)/shard_map/ppermute | solution.py:216
  129.2 12.6 %collective-permute-start.30 = (bf16[448,128]{1,0:T(8,128)(2,1)S(1)}, bf16[448,128]{1,0:T(8,128)(2,1)S(1)}, u32[]{:S(2)}, u32[]{:S(2)}) collective-permute-start(bf16[448,128]{1,0:T(8,128)(2,1)S(1)} %get-tuple-element.46), channel_id=1, source_target_pairs={{0,96},{16,112},{32,128},{48,144},{64,160},{80,176},{96,192},{112,... | collective-permute-start | bytes 344072 | tf_op jit(solution)/shard_map/ppermute | solution.py:216
  130.9 11.0 %collective-permute-start.31 = (bf16[448,128]{1,0:T(8,128)(2,1)S(1)}, bf16[448,128]{1,0:T(8,128)(2,1)S(1)}, u32[]{:S(2)}, u32[]{:S(2)}) collective-permute-start(bf16[448,128]{1,0:T(8,128)(2,1)S(1)} %get-tuple-element.47), channel_id=1, source_target_pairs={{0,64},{16,80},{32,96},{48,112},{64,128},{80,144},{96,160},{112,17... | collective-permute-start | bytes 344072 | tf_op jit(solution)/shard_map/ppermute | solution.py:216
  134.7 8.9 %collective-permute-start.26 = (bf16[448,128]{1,0:T(8,128)(2,1)S(1)}, bf16[448,128]{1,0:T(8,128)(2,1)S(1)}, u32[]{:S(2)}, u32[]{:S(2)}) collective-permute-start(bf16[448,128]{1,0:T(8,128)(2,1)S(1)} %get-tuple-element.40), channel_id=1, source_target_pairs={{0,224},{16,240},{32,0},{48,16},{64,32},{80,48},{96,64},{112,80},{... | collective-permute-start | bytes 344072 | tf_op jit(solution)/shard_map/ppermute | solution.py:216
  139.6 9.6 %collective-permute-start.29 = (bf16[448,128]{1,0:T(8,128)(2,1)S(1)}, bf16[448,128]{1,0:T(8,128)(2,1)S(1)}, u32[]{:S(2)}, u32[]{:S(2)}) collective-permute-start(bf16[448,128]{1,0:T(8,128)(2,1)S(1)} %get-tuple-element.45), channel_id=1, source_target_pairs={{0,128},{16,144},{32,160},{48,176},{64,192},{80,208},{96,224},{112... | collective-permute-start | bytes 344072 | tf_op jit(solution)/shard_map/ppermute | solution.py:216
  141.1 9.1 %collective-permute-start.32 = (bf16[448,128]{1,0:T(8,128)(2,1)S(1)}, bf16[448,128]{1,0:T(8,128)(2,1)S(1)}, u32[]{:S(2)}, u32[]{:S(2)}) collective-permute-start(bf16[448,128]{1,0:T(8,128)(2,1)S(1)} %get-tuple-element.48), channel_id=1, source_target_pairs={{0,32},{16,48},{32,64},{48,80},{64,96},{80,112},{96,128},{112,144}... | collective-permute-start | bytes 344072 | tf_op jit(solution)/shard_map/ppermute | solution.py:216
  151.5 6.5 %collective-permute-start.33 = (f32[128,448]{1,0:T(8,128)S(1)}, f32[128,448]{1,0:T(8,128)S(1)}, u32[]{:S(2)}, u32[]{:S(2)}) collective-permute-start(f32[128,448]{1,0:T(8,128)S(1)} %get-tuple-element.50), channel_id=1, source_target_pairs={{0,16},{16,0},{32,48},{48,32},{64,80},{80,64},{96,112},{112,96},{1... | collective-permute-start | bytes 688136 | tf_op jit(solution)/shard_map/ppermute | solution.py:212
